TPU v7x, 32 devices: a whole 2x2x4 slice. The times are simulated.
32 devices in a mesh: row: 8 (over z, x), feat: 4 (over y, core).
Axes of the slice: x: 2, y: 2, z: 4, core: 2. Of those that a mesh axis runs over, the one named last changes fastest.
Arguments:
- bin_codes: int32 [256, 65536], P(None, 'row'), may hold values from 0 to 31
- gradients: bfloat16 [65536], P('row'), may hold values from -6 to 6
- hessians: bfloat16 [65536], P('row'), may hold values from 0.019897461 to 0.25
- pair_list: int32 [64, 2], replicated, may hold values from 0 to 255, as said below
- owners: int32 [64], replicated, may hold values from 0 to 3, as said below
Outputs:
- cut_table: float32 [128, 1024], P('feat', 'row')
- best_gain: float32 [64], replicated
Inputs may be any that keep to these rules, and one draw needn't show every extreme that they name: `pair_list`: each row holds two different features, the first smaller. `owners`: one index owns exactly 32 pairs in every draw, the others at most that many.
All inputs are finite; a program needn't handle non-finite values.
Results may differ from a plain program's by a relative error of at most 0.0003.
Values sent between devices are 32-bit elements; how exact they have to be, the bound alone decides.
No kernel may reach another device: no remote copies, remote signals or barrier semaphores. Data moves between devices by JAX's collectives and lax.ppermute only.
A program may use at most 64 MiB of HBM per device.

v0:
```python
import jax
import jax.numpy as jnp
from jax import lax
from jax.sharding import PartitionSpec as P

BINS = 32


LAMBDA_REG = 1.0


def slot_rank(owners):
    pair_ids = jnp.arange(owners.shape[0], dtype=jnp.int32)
    same_owner = owners[:, None] == owners[None, :]
    earlier = pair_ids[None, :] < pair_ids[:, None]
    return jnp.sum((same_owner & earlier).astype(jnp.int32), axis=1)


def cumulate(histogram):
    bin_count = histogram.shape[-2]
    running = jnp.cumsum(histogram, axis=-2)
    shaped = running.reshape(running.shape[:-1] + (2, bin_count))
    shaped = jnp.cumsum(shaped, axis=-1)
    return shaped.reshape(running.shape)


def cut_gains(cut_rows, margin_row):
    bin_count = margin_row.shape[-1] // 2
    grad_cum = cut_rows[..., :bin_count]
    hess_cum = cut_rows[..., bin_count:]
    grad_end = grad_cum[..., -1:]
    hess_end = hess_cum[..., -1:]
    grad_col = margin_row[..., None, :bin_count]
    hess_col = margin_row[..., None, bin_count:]
    grad_all = margin_row[..., None, bin_count - 1 : bin_count]
    hess_all = margin_row[..., None, 2 * bin_count - 1 :]
    quad_grad = (
        grad_cum,
        grad_end - grad_cum,
        grad_col - grad_cum,
        grad_all - grad_end - grad_col + grad_cum,
    )
    quad_hess = (
        hess_cum,
        hess_end - hess_cum,
        hess_col - hess_cum,
        hess_all - hess_end - hess_col + hess_cum,
    )
    result = -(grad_all * grad_all) / (hess_all + LAMBDA_REG)
    for grad_part, hess_part in zip(quad_grad, quad_hess):
        result = result + grad_part * grad_part / (hess_part + LAMBDA_REG)
    return result


def shards(bin_codes, gradients, hessians, pair_list, owners):
    feat_count = lax.axis_size("feat")
    row_count = lax.axis_size("row")
    feat_index = lax.axis_index("feat")
    row_index = lax.axis_index("row")
    pair_count = pair_list.shape[0]
    bin_count = BINS
    row_share = bin_count // row_count
    home_slots = 2 * pair_count // feat_count
    rank = slot_rank(owners)
    pair_ids = jnp.arange(pair_count, dtype=jnp.int32)
    slot_count = pair_count // feat_count
    chosen = jnp.arange(slot_count, dtype=jnp.int32) * feat_count + feat_index
    present = jnp.ones((slot_count,), dtype=bool)
    lookup = pair_ids % feat_count * slot_count + pair_ids // feat_count
    chosen_pairs = pair_list[chosen]
    picked = jnp.take(bin_codes, chosen_pairs.reshape(-1), axis=0)
    picked = picked.reshape(slot_count, 2, -1)
    levels = jnp.arange(bin_count, dtype=jnp.int32)
    hot_first = (picked[:, 0, None, :] == levels[None, :, None]).astype(jnp.bfloat16)
    hot_second = (picked[:, 1, None, :] == levels[None, :, None]).astype(jnp.bfloat16)
    weighted = jnp.concatenate(
        [hot_second * gradients[None, None, :], hot_second * hessians[None, None, :]], axis=1
    )
    histogram = jnp.einsum("sar,sxr->sax", hot_first, weighted, preferred_element_type=jnp.float32)
    histogram = histogram * present[:, None, None].astype(jnp.float32)
    summed = lax.psum(histogram, "row")
    running = cumulate(summed)
    cut_rows = lax.dynamic_slice_in_dim(running, row_index * row_share, row_share, 1)
    margin_row = running[:, -1, :]
    cut_gain = cut_gains(cut_rows, margin_row).reshape(slot_count, row_share * bin_count)
    row_peak = lax.pmax(jnp.max(cut_gain, axis=1), "row")
    everyone = lax.all_gather(row_peak, "feat", axis=0, tiled=True)
    best_gain = everyone[lookup]
    own_pairs = jnp.arange(slot_count, dtype=jnp.int32) * feat_count + feat_index
    targets = jnp.arange(feat_count, dtype=jnp.int32)
    home_places = jnp.arange(home_slots, dtype=jnp.int32)
    routed = (owners[own_pairs][None, None, :] == targets[:, None, None]) & (
        rank[own_pairs][None, None, :] == home_places[None, :, None]
    )
    local_ids = jnp.arange(slot_count, dtype=jnp.int32)
    source = jnp.sum(jnp.where(routed, local_ids[None, None, :], 0), axis=2)
    has_pair = jnp.any(routed, axis=2)
    outgoing = jnp.where(has_pair[:, :, None], cut_gain[source], jnp.float32(0.0))
    incoming = lax.all_to_all(outgoing, "feat", split_axis=0, concat_axis=0, tiled=True)
    cut_table = jnp.sum(incoming, axis=0)
    return (cut_table, best_gain)


def solution(mesh):
    in_specs = (P(None, "row"), P("row"), P("row"), P(), P())
    out_specs = (P("feat", "row"), P())
    return jax.shard_map(shards, mesh=mesh, in_specs=in_specs, out_specs=out_specs, check_vma=False)
```

profile of v0, /device:TPU:0, one launch (start us, length us, event | category | flops | bytes accessed | tf_op | source)
XLA Modules:
  0.0 159.0 jit_solution(3838328984315650092)
XLA Ops:
  7.2 0.0 all-reduce.3.cloned.1.call-start
  7.3 0.8 copy.64
  8.0 0.6 gather_fusion.2
  8.6 0.1 reshape.228
  8.7 4.7 %gather_fusion.3 = s32[32,8192]{1,0:T(8,128)S(1)} fusion(s32[256,8192]{1,0:T(8,128)} %param.5, s32[1024]{0:T(1024)S(1)} %pad_clamp_fusion.2), kind=kCustom, calls=%fused_computation.3 | custom fusion | bytes 2097280 | tf_op jit(solution)/shard_map/jit(_take)/gather | solution.py:71
  13.5 0.6 gather.25
  14.1 0.1 copy.65
  14.2 0.7 copy_select_fusion
  14.9 0.1 slice_bitcast_fusion.1
  15.0 9.2 %fusion.5 = (bf16[16,32,8192]{2,1,0:T(8,128)(2,1)}, bf16[16,32,8192]{2,1,0:T(8,128)(2,1)}) fusion(s32[16,8192]{1,0:T(8,128)S(1)} %get-tuple-element.7, bf16[8192]{0:T(1024)(128)(2,1)S(1)} %copy-done.1, bf16[8192]{0:T(1024)(128)(2,1)S(1)} %copy-done.2), kind=kLoop, calls=%fused_computation.12 | loop fusion | flops 12582912 | bytes 17334272 | tf_op jit(solution)/shard_map/mul | solution.py:77
  24.2 8.3 %fusion = f32[16,32,64]{2,1,0:T(8,128)S(1)} fusion(bf16[16,32,8192]{2,1,0:T(8,128)(2,1)} %get-tuple-element.9, bf16[16,32,8192]{2,1,0:T(8,128)(2,1)} %get-tuple-element.8, s32[16,8192]{1,0:T(8,128)S(1)} %get-tuple-element.6), kind=kOutput, calls=%fused_computation.6 | convolution fusion | flops 574619648 | bytes 17432576 | tf_op jit(solution)/shard_map/sar,sxr->sax/dot_general | solution.py:79
  32.5 0.3 reduce_window_sum.24
  32.8 1.1 copy.67
  34.0 0.2 convert_reduce_fusion
  34.2 0.7 gather_fusion
  34.8 0.7 gather_fusion.1
  35.5 0.1 iota_compare_fusion.4
  35.6 0.1 fusion.7
  35.7 0.1 reshape.265
  35.8 0.1 and_reduce_fusion
  35.9 73.3 %all-reduce.3.cloned.1.call-done = f32[16,32,2,32]{3,0,1,2:T(8,128)} async-done(((f32[16,32,2,32]{3,0,1,2:T(8,128)}), f32[16,32,2,32]{3,0,1,2:T(8,128)}) %all-reduce.3.cloned.1.call-update) | async-done | bytes 131088 | tf_op jit(solution)/shard_map/psum | solution.py:81
  109.2 1.1 fusion.17
  110.3 0.2 copy.68
  110.5 6.1 %reduce_window_sum.26 = f32[16,32,2,32]{3,1,2,0:T(8,128)S(1)} reduce-window(f32[16,32,2,32]{3,1,2,0:T(8,128)S(1)} %copy.68, f32[]{:T(128)} %constant.75.clone.1), window={size=1x1x1x32 pad=0_0x0_0x0_0x31_0}, to_apply=%region_4.5 | reduce-window | flops 1015808 | bytes 262148 | tf_op jit(solution)/shard_map/jit(cumsum)/reduce_window_sum | solution.py:23
  116.6 0.4 copy.69
  117.1 0.3 reshape.229
  117.4 0.2 slice_reduce_fusion.1
  117.6 0.1 fusion.16
  117.6 0.1 constant_dynamic-slice_fusion
  117.8 0.1 copy.77
  117.9 0.1 copy.78
  118.0 0.1 constant_dynamic-slice_fusion.2
  118.1 0.1 copy.75
  118.2 0.1 copy.76
  118.3 0.1 copy.71
  118.3 0.1 copy.72
  118.4 0.2 fusion.15
  118.6 0.1 copy.73
  118.7 0.1 reshape.230
  118.8 0.6 gather_fusion.4
  119.4 0.7 broadcast_select_fusion
  120.1 3.3 %all-to-all-start = ((f32[4,32,128]{2,1,0:T(8,128)}), f32[4,32,128]{2,1,0:T(8,128)S(1)}, u32[]{:S(2)}, u32[]{:S(2)}) async-start(f32[4,32,128]{2,1,0:T(8,128)} %broadcast_select_fusion), calls=%async_computation | async-start | bytes 131072 | tf_op jit(solution)/shard_map/all_to_all | solution.py:99
  123.4 0.6 dynamic-slice
  124.7 19.7 %pmax.7 = f32[16]{0:T(128)S(1)} all-reduce(f32[16]{0:T(128)S(1)} %get-tuple-element.4), channel_id=1, replica_groups=mesh['row'=8,'feat'=4] {'row'}, use_global_device_ids=true, to_apply=%region_8.9 | all-reduce | flops 16 | bytes 128 | tf_op jit(solution)/shard_map/pmax | solution.py:86
  144.4 0.2 dynamic-update-slice
  144.6 5.6 %all-reduce = f32[64]{0:T(128)S(1)} all-reduce(f32[64]{0:T(128)S(1)} %dynamic-update-slice), channel_id=1, replica_groups=mesh['row'=8,'feat'=4] {'feat'}, use_global_device_ids=true, to_apply=%add | all-reduce | flops 64 | bytes 512
  150.3 1.3 gather_fusion.5
  151.6 0.6 reduce_sum.32
  (24 shorter events, 0.1 us)
Async XLA Ops:
  7.2 7.8 %copy-start.1 = (bf16[8192]{0:T(1024)(128)(2,1)S(1)}, bf16[8192]{0:T(1024)(128)(2,1)}, u32[]{:S(2)}) copy-start(bf16[8192]{0:T(1024)(128)(2,1)} %param.6) | copy-start | bytes 49156
  7.2 7.8 %copy-start.2 = (bf16[8192]{0:T(1024)(128)(2,1)S(1)}, bf16[8192]{0:T(1024)(128)(2,1)}, u32[]{:S(2)}) copy-start(bf16[8192]{0:T(1024)(128)(2,1)} %param.7) | copy-start | bytes 49156
  7.2 102.1 %all-reduce.3.cloned.1.call-start = ((), (), s32[]{:S(2)}) async-start(), calls=%async_computation.1 | async-start | bytes 1048576 | tf_op jit(solution)/shard_map/psum | solution.py:81
  24.2 9.8 %copy-start = (s32[64]{0:T(128)S(1)}, s32[64]{0:T(128)}, u32[]{:S(2)}) copy-start(s32[64]{0:T(128)} %param.9) | copy-start | bytes 772
  32.5 90.9 %copy-start.3 = (u32[32]{0:T(128)S(1)}, u32[32]{0:T(128)}, u32[]{:S(2)}) copy-start(u32[32]{0:T(128)} %constant.88) | copy-start | bytes 388
  120.1 31.4 %all-to-all-start = ((f32[4,32,128]{2,1,0:T(8,128)}), f32[4,32,128]{2,1,0:T(8,128)S(1)}, u32[]{:S(2)}, u32[]{:S(2)}) async-start(f32[4,32,128]{2,1,0:T(8,128)} %broadcast_select_fusion), calls=%async_computation | async-start | bytes 131072 | tf_op jit(solution)/shard_map/all_to_all | solution.py:99
Sparse Core Ops, SparseCore 0:
  34.1 75.0 all-reduce.2
where the time goes:
time: 159 us
  waiting for transfers between devices  73.4 us (46%)
  blocking collectives  25.4 us (16%)
  other arithmetic  19.1 us (12%)
  between operations  14.9 us (9%)
  local copies, waits for them, and re-layouts  14.6 us (9%)
  matrix products  8.33 us (5%)
  starting transfers between devices  3.32 us (2%)
    psum x1, waiting for transfers between devices, shards(): summed = lax.psum(histogram, 'row')  73.3 us
    pmax x1, blocking collectives, shards(): row_peak = lax.pmax(jnp.max(cut_gain, axis=1), 'row')  19.7 us
    mul x1, other arithmetic, shards(): hot_second * gradients[None, None, :]  9.18 us
    dot_general x1, matrix products, shards(): jnp.einsum('sar,sxr->sax', hot_first, weighted, preferred_element_type=jn...  8.33 us
    another operation x1, other arithmetic, cumulate(): shaped = jnp.cumsum(shaped, axis=-1)  6.13 us
    unnamed x1, blocking collectives  5.63 us
    gather x2, local copies, waits for them, and re-layouts, shards(): picked = jnp.take(bin_codes, chosen_pairs.reshape(-1), axis=0)  5.36 us
    all_to_all x1, starting transfers between devices, shards(): lax.all_to_all(outgoing, 'feat', split_axis=0, concat_axis=0, tiled=True)  3.28 us
  transfers between devices with their start and end apart: 2, of which 1 were waited for; matrix products, arithmetic and copies ran while one was open for 3% of the time, Pallas kernels for 0%

commit v1 on v0

v1 whole, which is shorter than its diff:
```python
import functools

import jax
import jax.numpy as jnp
from jax import lax
from jax.experimental import pallas as pl
from jax.experimental.pallas import tpu as pltpu
from jax.sharding import PartitionSpec as P

BINS = 32
LAMBDA_REG = 1.0
LANES = 128
GROUP = 4
PER_MESSAGE = 2
PARTS = 4
CHUNK = 2048


def cut_sums_kernel(feat_slots, pairs_hbm, codes_hbm, grad_hbm, hess_hbm, out_ref, pairs, codes, grad, hess, grad_wide, hess_wide, sums, code_sems, small_sems):
    groups = feat_slots // GROUP
    first_pair = lax.axis_index("feat") * feat_slots
    row_count = codes.shape[1]
    pairs_copy = pltpu.make_async_copy(pairs_hbm, pairs, small_sems.at[0])
    grad_copy = pltpu.make_async_copy(grad_hbm, grad, small_sems.at[1])
    hess_copy = pltpu.make_async_copy(hess_hbm, hess, small_sems.at[2])
    pairs_copy.start()
    grad_copy.start()
    hess_copy.start()
    pairs_copy.wait()
    code_copies = []
    for slot in range(feat_slots):
        for side in range(2):
            line = 2 * slot + side
            copy = pltpu.make_async_copy(
                codes_hbm.at[pl.ds(pairs[side, first_pair + slot], 1)], codes.at[pl.ds(line, 1)], code_sems.at[line]
            )
            copy.start()
            code_copies.append(copy)
    sums[...] = jnp.zeros_like(sums)
    half = BINS // 2
    levels = lax.broadcasted_iota(jnp.int32, (half, 1), 0).astype(jnp.float32)
    level_parts = (levels.astype(jnp.bfloat16), (levels + half).astype(jnp.bfloat16))
    grad_copy.wait()
    hess_copy.wait()
    for narrow, wide in ((grad, grad_wide), (hess, hess_wide)):
        values = narrow[...].astype(jnp.float32)
        for tile in range(row_count // LANES):
            line = jnp.broadcast_to(values[tile : tile + 1], (half, LANES))
            wide[:, tile * LANES : (tile + 1) * LANES] = line.astype(jnp.bfloat16)
    zero = jnp.zeros((half, CHUNK), jnp.bfloat16)
    one = jnp.ones((half, CHUNK), jnp.bfloat16)
    for copy in code_copies:
        copy.wait()

    def spread(line, span):
        values = codes[pl.ds(line, 1), span].astype(jnp.float32)
        return jnp.broadcast_to(values, (half, CHUNK)).astype(jnp.bfloat16)

    def step(index, carry):
        span = pl.ds(pl.multiple_of(index * CHUNK, CHUNK), CHUNK)
        grad_part = grad_wide[:, span]
        hess_part = hess_wide[:, span]
        for group in range(groups):
            grad_rows, hess_rows, second_rows = [], [], []
            for pair in range(GROUP):
                line = 2 * (GROUP * group + pair)
                first = spread(line, span)
                second = spread(line + 1, span)
                for level in level_parts:
                    below = first <= level
                    grad_rows.append(jnp.where(below, grad_part, zero))
                    hess_rows.append(jnp.where(below, hess_part, zero))
                    second_rows.append(jnp.where(second <= level, one, zero))
            weighted = jnp.concatenate(grad_rows + hess_rows, axis=0)
            hot = jnp.concatenate(second_rows, axis=0)
            sums[group] += lax.dot_general(
                weighted, hot, (((1,), (1,)), ((), ())), preferred_element_type=jnp.float32
            )
        return carry

    lax.fori_loop(0, row_count // CHUNK, step, 0)
    lane = lax.broadcasted_iota(jnp.int32, (BINS, LANES), 1)
    low = lane < LANES // 2

    def own_blocks(group, start):
        block = sums[group, start : start + BINS]
        for pair in range(1, GROUP):
            at = start + pair * BINS
            block = jnp.where(lane >= pair * BINS, sums[group, at : at + BINS], block)
        return block

    for group in range(groups):
        grad_cum = own_blocks(group, 0)
        hess_cum = own_blocks(group, GROUP * BINS)
        out_ref[2 * group] = jnp.where(low, grad_cum, pltpu.roll(hess_cum, LANES // 2, 1))
        out_ref[2 * group + 1] = jnp.where(low, pltpu.roll(grad_cum, LANES // 2, 1), hess_cum)
    for message in range(2 * groups, out_ref.shape[0]):
        out_ref[message] = jnp.zeros((BINS, LANES), jnp.float32)


def cut_sums(bin_codes, gradients, hessians, pair_list, feat_slots, messages):
    row_count = bin_codes.shape[1]
    groups = feat_slots // GROUP
    tiles = row_count // LANES
    anywhere = pl.BlockSpec(memory_space=pl.ANY)
    return pl.pallas_call(
        functools.partial(cut_sums_kernel, feat_slots),
        out_shape=jax.ShapeDtypeStruct((messages, BINS, LANES), jnp.float32),
        in_specs=[anywhere] * 4,
        out_specs=pl.BlockSpec(memory_space=pltpu.VMEM),
        scratch_shapes=[
            pltpu.SMEM((2, pair_list.shape[0]), jnp.int32),
            pltpu.VMEM((2 * feat_slots, row_count), jnp.int32),
            pltpu.VMEM((tiles, LANES), jnp.bfloat16),
            pltpu.VMEM((tiles, LANES), jnp.bfloat16),
            pltpu.VMEM((BINS // 2, row_count), jnp.bfloat16),
            pltpu.VMEM((BINS // 2, row_count), jnp.bfloat16),
            pltpu.VMEM((groups, 2 * GROUP * BINS, GROUP * BINS), jnp.float32),
            pltpu.SemaphoreType.DMA((2 * feat_slots,)),
            pltpu.SemaphoreType.DMA((3,)),
        ],
        compiler_params=pltpu.CompilerParams(vmem_limit_bytes=56 * 2**20),
    )(pair_list.T, bin_codes, gradients.reshape(tiles, LANES), hessians.reshape(tiles, LANES))


def gains_kernel(feat_slots, parts_ref, out_ref, gains):
    row_count, feat_count = out_ref.shape[0], out_ref.shape[1]
    share = BINS // row_count
    total = parts_ref[0]
    for part in range(1, parts_ref.shape[0]):
        total = total + parts_ref[part]
    lane = lax.broadcasted_iota(jnp.int32, (BINS, LANES), 1)
    first_half = lane < BINS

    def ends(cum):
        return jnp.where(first_half, cum[:, BINS - 1 : BINS], cum[:, 2 * BINS - 1 : 2 * BINS])

    grad_cum = total
    hess_cum = pltpu.roll(total, LANES // 2, 1)
    grad_end, hess_end = ends(grad_cum), ends(hess_cum)
    grad_col, hess_col = grad_cum[BINS - 1 :], hess_cum[BINS - 1 :]
    grad_all, hess_all = grad_end[BINS - 1 :], hess_end[BINS - 1 :]
    result = -(grad_all * grad_all) / (hess_all + LAMBDA_REG)
    for grad_part, hess_part in (
        (grad_cum, hess_cum),
        (grad_end - grad_cum, hess_end - hess_cum),
        (grad_col - grad_cum, hess_col - hess_cum),
        (grad_all - grad_end - grad_col + grad_cum, hess_all - hess_end - hess_col + hess_cum),
    ):
        result = result + grad_part * grad_part / (hess_part + LAMBDA_REG)
    gains[...] = result
    peak = jnp.max(result, axis=0, keepdims=True)
    line = lax.broadcasted_iota(jnp.int32, (1, LANES), 1)
    row_index = lax.axis_index("row")
    first_pair = lax.axis_index("feat") * feat_slots + PER_MESSAGE * row_index
    held = row_index < feat_slots // PER_MESSAGE
    best = jnp.zeros((1, LANES), jnp.float32)
    for pair in range(PER_MESSAGE):
        inside = (line >= pair * BINS) & (line < (pair + 1) * BINS)
        top = jnp.max(jnp.where(inside, peak, -jnp.inf), axis=1, keepdims=True)
        best = jnp.where((line == first_pair + pair) & held, top, best)
    wide = lax.broadcasted_iota(jnp.int32, (row_count, LANES), 1)
    cuts = []
    for pair in range(PER_MESSAGE):
        laid = jnp.zeros((row_count, LANES), jnp.float32)
        for step in range(share):
            lines = gains[pl.ds(step, row_count, stride=share), :] if share > 1 else gains[...]
            moved = (step - pair) * BINS % LANES
            if moved:
                lines = pltpu.roll(lines, moved, 1)
            laid = jnp.where((wide >= step * BINS) & (wide < (step + 1) * BINS), lines, laid)
        cuts.append(laid)
    spot = lax.broadcasted_iota(jnp.int32, (PARTS, LANES), 0)
    for row in range(row_count):
        message = jnp.where(spot == 0, cuts[0][row : row + 1], jnp.where(spot == 1, cuts[1][row : row + 1], best))
        for feat in range(feat_count):
            out_ref[row, feat] = message


def table_kernel(feat_slots, feat_count, owners_ref, parts_ref, table_ref, best_ref, table):
    feat_index = lax.axis_index("feat")
    home_slots, width = table_ref.shape
    table[...] = jnp.zeros_like(table)
    taken = jnp.int32(0)
    for pair in range(owners_ref.shape[0]):
        place = pair % feat_slots
        source = place // PER_MESSAGE * feat_count + pair // feat_slots
        mine = owners_ref[pair] == feat_index
        slot = jnp.where(mine, jnp.minimum(taken, home_slots), home_slots)
        table[pl.ds(slot, 1), :] = parts_ref[source, place % PER_MESSAGE : place % PER_MESSAGE + 1, :]
        taken = taken + mine.astype(jnp.int32)
    table_ref[...] = table[:home_slots, :width]
    best = jnp.sum(parts_ref[:, PER_MESSAGE, :], axis=0, keepdims=True)
    best_ref[...] = best[:, : best_ref.shape[1]]


def shards(bin_codes, gradients, hessians, pair_list, owners):
    feat_count = lax.axis_size("feat")
    row_count = lax.axis_size("row")
    pair_count = pair_list.shape[0]
    feat_slots = pair_count // feat_count
    home_slots = 2 * pair_count // feat_count
    width = BINS // row_count * BINS
    in_vmem = pl.BlockSpec(memory_space=pltpu.VMEM)
    partial = cut_sums(bin_codes, gradients, hessians, pair_list, feat_slots, row_count)
    parts = lax.all_to_all(partial, "row", split_axis=0, concat_axis=0, tiled=True)
    outgoing = pl.pallas_call(
        functools.partial(gains_kernel, feat_slots),
        out_shape=jax.ShapeDtypeStruct((row_count, feat_count, PARTS, LANES), jnp.float32),
        in_specs=[in_vmem],
        out_specs=in_vmem,
        scratch_shapes=[pltpu.VMEM((BINS, LANES), jnp.float32)],
    )(parts)
    outgoing = outgoing.reshape(row_count * feat_count, PARTS, LANES)
    incoming = lax.all_to_all(outgoing, ("row", "feat"), split_axis=0, concat_axis=0, tiled=True)
    cut_table, best = pl.pallas_call(
        functools.partial(table_kernel, feat_slots, feat_count),
        out_shape=(
            jax.ShapeDtypeStruct((home_slots, width), jnp.float32),
            jax.ShapeDtypeStruct((1, pair_count), jnp.float32),
        ),
        in_specs=[pl.BlockSpec(memory_space=pltpu.SMEM), in_vmem],
        out_specs=(in_vmem, in_vmem),
        scratch_shapes=[pltpu.VMEM((home_slots + 8, LANES), jnp.float32)],
    )(owners, incoming)
    return (cut_table, best.reshape(pair_count))


def solution(mesh):
    in_specs = (P(None, "row"), P("row"), P("row"), P(), P())
    out_specs = (P("feat", "row"), P())
    return jax.shard_map(shards, mesh=mesh, in_specs=in_specs, out_specs=out_specs, check_vma=False)
```

time: 159 us -> 37.9 us (0.24)
  waiting for transfers between devices: 73.4 us -> 0 us
  other arithmetic: 19.1 us -> 0 us
  local copies, waits for them, and re-layouts: 14.6 us -> 0 us
  between operations: 14.9 us -> 0.64 us
  Pallas kernels: 0 us -> 11.4 us
  matrix products: 8.33 us -> 0 us
  starting transfers between devices: 3.32 us -> 0 us
    psum x1 -> x0, waiting for transfers between devices: 73.3 us -> none  [shards(): summed = lax.psum(histogram, 'row')]
    all_to_all x0 -> x2, blocking collectives: none -> 25.4 us  [the longest x1 14.7 us: shards(): lax.all_to_all(partial, 'row', split_axis=0, concat_axis=0, tiled=True)]
    pmax x1 -> x0, blocking collectives: 19.7 us -> none  [shards(): row_peak = lax.pmax(jnp.max(cut_gain, axis=1), 'row')]
    pallas_call x0 -> x3, Pallas kernels: none -> 11.4 us  [the longest x1 7.98 us: cut_sums(): pl.pallas_call(functools.partial(cut_sums_kernel, feat_slots), out_shape=...]
    gather x7 -> x0, local copies, waits for them, and re-layouts: 9.19 us -> none  [the longest x2 5.36 us: shards(): picked = jnp.take(bin_codes, chosen_pairs.reshape(-1), axis=0)]
    mul x1 -> x0, other arithmetic: 9.18 us -> none  [shards(): hot_second * gradients[None, None, :]]
    dot_general x1 -> x0, matrix products: 8.33 us -> none  [shards(): jnp.einsum('sar,sxr->sax', hot_first, weighted, preferred_element_type=jn...]
    another operation x2 -> x0, other arithmetic: 7.22 us -> none  [the longest x1 6.13 us: cumulate(): shaped = jnp.cumsum(shaped, axis=-1)]
  transfers between devices with their start and end apart: 2 -> 0, of which waited for: 1 -> 0; matrix products, arithmetic and copies ran while one was open for 3% -> 0% of each run, Pallas kernels for 0% -> 0%
where the time goes in v1:
time: 37.9 us; the launch traced here: 37.4 us
  blocking collectives  25.4 us (67%)
  Pallas kernels  11.4 us (30%)
  between operations  0.64 us (2%)
    all_to_all x1, blocking collectives, shards(): lax.all_to_all(partial, 'row', split_axis=0, concat_axis=0, tiled=True)  14.7 us
    all_to_all x1, blocking collectives, shards(): lax.all_to_all(outgoing, ('row', 'feat'), split_axis=0, concat_axis=0, ti...  10.7 us
    pallas_call x1, Pallas kernels, cut_sums(): pl.pallas_call(functools.partial(cut_sums_kernel, feat_slots), out_shape=...  7.98 us
    pallas_call x1, Pallas kernels, shards(): pl.pallas_call(functools.partial(gains_kernel, feat_slots), out_shape=jax...  1.82 us
    pallas_call x1, Pallas kernels, shards(): pl.pallas_call(functools.partial(table_kernel, feat_slots, feat_count), o...  1.62 us

profile of v1, /device:TPU:0, one launch (start us, length us, event | category | flops | bytes accessed | tf_op | source)
XLA Modules:
  0.0 37.4 jit_solution(11099104882215171399)
XLA Ops:
  0.6 8.0 %shard_map.68 = f32[8,32,128]{2,1,0:T(8,128)} custom-call(s32[2,64]{1,0:T(2,128)} %bitcast.8, s32[256,8192]{1,0:T(8,128)} %codes_hbm.1, bf16[64,128]{1,0:T(8,128)(2,1)} %bitcast.6, bf16[64,128]{1,0:T(8,128)(2,1)} %bitcast.7), custom_call_target="tpu_custom_call" | custom-call | tf_op jit(solution)/shard_map/pallas_call | solution.py:106
  8.6 14.7 %all_to_all.10.parts_ref = f32[8,32,128]{2,1,0:T(8,128)} all-to-all(f32[8,32,128]{2,1,0:T(8,128)} %shard_map.68), channel_id=1, replica_groups=mesh['row'=8,'feat'=4] {'row'}, dimensions={0} | all-to-all | bytes 262144 | tf_op jit(solution)/shard_map/all_to_all | solution.py:206
  23.3 1.8 %shard_map.69 = f32[8,4,4,128]{3,2,1,0:T(4,128)} custom-call(f32[8,32,128]{2,1,0:T(8,128)} %all_to_all.10.parts_ref), custom_call_target="tpu_custom_call" | custom-call | tf_op jit(solution)/shard_map/pallas_call | solution.py:207
  25.1 10.7 %all_to_all.11.parts_ref = f32[32,4,128]{2,1,0:T(4,128)} all-to-all(f32[32,4,128]{2,1,0:T(4,128)} %bitcast.5), channel_id=1, replica_groups=mesh['row'=8,'feat'=4] {'row','feat'}, dimensions={0} | all-to-all | bytes 131072 | tf_op jit(solution)/shard_map/all_to_all | solution.py:215
  35.8 1.6 %shard_map.70 = (f32[32,128]{1,0:T(8,128)}, f32[1,64]{1,0:T(1,128)}) custom-call(s32[64]{0:T(128)} %owners_ref.1, f32[32,4,128]{2,1,0:T(4,128)} %all_to_all.11.parts_ref), custom_call_target="tpu_custom_call" | custom-call | tf_op jit(solution)/shard_map/pallas_call | solution.py:216

commit v2 on v1

--- a/solution.py
+++ b/solution.py
@@ -14,6 +14,8 @@
 PER_MESSAGE = 2
 PARTS = 4
 CHUNK = 2048
+SUMS_VMEM = 24 * 2**20
+SMALL_VMEM = 4 * 2**20
 
 
 def cut_sums_kernel(feat_slots, pairs_hbm, codes_hbm, grad_hbm, hess_hbm, out_ref, pairs, codes, grad, hess, grad_wide, hess_wide, sums, code_sems, small_sems):
@@ -103,6 +105,7 @@
     groups = feat_slots // GROUP
     tiles = row_count // LANES
     anywhere = pl.BlockSpec(memory_space=pl.ANY)
+    operands = (pair_list.T, bin_codes, gradients.reshape(tiles, LANES), hessians.reshape(tiles, LANES))
     return pl.pallas_call(
         functools.partial(cut_sums_kernel, feat_slots),
         out_shape=jax.ShapeDtypeStruct((messages, BINS, LANES), jnp.float32),
@@ -119,8 +122,8 @@
             pltpu.SemaphoreType.DMA((2 * feat_slots,)),
             pltpu.SemaphoreType.DMA((3,)),
         ],
-        compiler_params=pltpu.CompilerParams(vmem_limit_bytes=56 * 2**20),
-    )(pair_list.T, bin_codes, gradients.reshape(tiles, LANES), hessians.reshape(tiles, LANES))
+        compiler_params=pltpu.CompilerParams(vmem_limit_bytes=SUMS_VMEM),
+    )(*(pltpu.with_memory_space_constraint(operand, pltpu.HBM) for operand in operands))
 
 
 def gains_kernel(feat_slots, parts_ref, out_ref, gains):
@@ -210,6 +213,7 @@
         in_specs=[in_vmem],
         out_specs=in_vmem,
         scratch_shapes=[pltpu.VMEM((BINS, LANES), jnp.float32)],
+        compiler_params=pltpu.CompilerParams(vmem_limit_bytes=SMALL_VMEM),
     )(parts)
     outgoing = outgoing.reshape(row_count * feat_count, PARTS, LANES)
     incoming = lax.all_to_all(outgoing, ("row", "feat"), split_axis=0, concat_axis=0, tiled=True)
@@ -222,6 +226,7 @@
         in_specs=[pl.BlockSpec(memory_space=pltpu.SMEM), in_vmem],
         out_specs=(in_vmem, in_vmem),
         scratch_shapes=[pltpu.VMEM((home_slots + 8, LANES), jnp.float32)],
+        compiler_params=pltpu.CompilerParams(vmem_limit_bytes=SMALL_VMEM),
     )(owners, incoming)
     return (cut_table, best.reshape(pair_count))
 

time: 37.9 us -> 34.1 us (0.90)
  Pallas kernels: 11.4 us -> 9.06 us
  blocking collectives: 25.4 us -> 24 us
    pallas_call x1, Pallas kernels: 1.82 us -> 0.28 us  [shards(): pl.pallas_call(functools.partial(gains_kernel, feat_slots), out_shape=jax...]
    all_to_all x1, blocking collectives: 10.7 us -> 9.63 us  [shards(): lax.all_to_all(outgoing, ('row', 'feat'), split_axis=0, concat_axis=0, ti...]
    pallas_call x1, Pallas kernels: 7.98 us -> 7.46 us  [cut_sums(): pl.pallas_call(functools.partial(cut_sums_kernel, feat_slots), out_shape=...]
where the time goes in v2:
time: 34.1 us; the launch traced here: 33.7 us
  blocking collectives  24 us (70%)
  Pallas kernels  9.06 us (27%)
  between operations  0.66 us (2%)
    all_to_all x1, blocking collectives, shards(): lax.all_to_all(partial, 'row', split_axis=0, concat_axis=0, tiled=True)  14.4 us
    all_to_all x1, blocking collectives, shards(): lax.all_to_all(outgoing, ('row', 'feat'), split_axis=0, concat_axis=0, ti...  9.63 us
    pallas_call x1, Pallas kernels, cut_sums(): pl.pallas_call(functools.partial(cut_sums_kernel, feat_slots), out_shape=...  7.46 us
    pallas_call x1, Pallas kernels, shards(): pl.pallas_call(functools.partial(table_kernel, feat_slots, feat_count), o...  1.31 us

profile of v2, /device:TPU:0, one launch (start us, length us, event | category | flops | bytes accessed | tf_op | source)
XLA Modules:
  0.0 33.7 jit_solution(1842110013326191182)
XLA Ops:
  0.6 0.0 copy-start
  0.6 7.5 %shard_map.68 = f32[8,32,128]{2,1,0:T(8,128)S(1)} custom-call(s32[2,64]{1,0:T(2,128)} %bitcast.8, s32[256,8192]{1,0:T(8,128)} %codes_hbm.1, bf16[64,128]{1,0:T(8,128)(2,1)} %bitcast.6, bf16[64,128]{1,0:T(8,128)(2,1)} %bitcast.7), custom_call_target="tpu_custom_call" | custom-call | tf_op jit(solution)/shard_map/pallas_call | solution.py:109
  8.1 14.4 %all_to_all.10.parts_ref = f32[8,32,128]{2,1,0:T(8,128)S(1)} all-to-all(f32[8,32,128]{2,1,0:T(8,128)S(1)} %shard_map.68), channel_id=1, replica_groups=mesh['row'=8,'feat'=4] {'row'}, dimensions={0} | all-to-all | bytes 262144 | tf_op jit(solution)/shard_map/all_to_all | solution.py:209
  22.5 0.3 shard_map.69
  22.8 9.6 %all_to_all.11.parts_ref = f32[32,4,128]{2,1,0:T(4,128)S(1)} all-to-all(f32[32,4,128]{2,1,0:T(4,128)S(1)} %bitcast.5), channel_id=1, replica_groups=mesh['row'=8,'feat'=4] {'row','feat'}, dimensions={0} | all-to-all | bytes 131072 | tf_op jit(solution)/shard_map/all_to_all | solution.py:219
  32.4 0.0 copy-done
  32.4 1.3 %shard_map.70 = (f32[32,128]{1,0:T(8,128)}, f32[1,64]{1,0:T(1,128)}) custom-call(s32[64]{0:T(128)S(1)} %copy-done, f32[32,4,128]{2,1,0:T(4,128)S(1)} %all_to_all.11.parts_ref), custom_call_target="tpu_custom_call" | custom-call | tf_op jit(solution)/shard_map/pallas_call | solution.py:220
Async XLA Ops:
  0.6 31.8 %copy-start = (s32[64]{0:T(128)S(1)}, s32[64]{0:T(128)}, u32[]{:S(2)}) copy-start(s32[64]{0:T(128)} %owners_ref.1) | copy-start | bytes 772

commit v3 on v2

--- a/solution.py
+++ b/solution.py
@@ -13,15 +13,16 @@
 GROUP = 4
 PER_MESSAGE = 2
 PARTS = 4
-CHUNK = 2048
-SUMS_VMEM = 24 * 2**20
+CHUNK = 4096
+SUMS_VMEM = 40 * 2**20
 SMALL_VMEM = 4 * 2**20
 
 
-def cut_sums_kernel(feat_slots, pairs_hbm, codes_hbm, grad_hbm, hess_hbm, out_ref, pairs, codes, grad, hess, grad_wide, hess_wide, sums, code_sems, small_sems):
+def cut_sums_kernel(feat_slots, pairs_hbm, codes_hbm, grad_hbm, hess_hbm, out_ref, pairs, codes, grad, hess, grad_tall, hess_tall, sums, code_sems, small_sems):
     groups = feat_slots // GROUP
     first_pair = lax.axis_index("feat") * feat_slots
     row_count = codes.shape[1]
+    chunks = row_count // CHUNK
     pairs_copy = pltpu.make_async_copy(pairs_hbm, pairs, small_sems.at[0])
     grad_copy = pltpu.make_async_copy(grad_hbm, grad, small_sems.at[1])
     hess_copy = pltpu.make_async_copy(hess_hbm, hess, small_sems.at[2])
@@ -29,71 +30,69 @@
     grad_copy.start()
     hess_copy.start()
     pairs_copy.wait()
+
+    def code_copy(feature, line):
+        return pltpu.make_async_copy(
+            codes_hbm.at[pl.ds(feature, 1)], codes.at[pl.ds(line, 1)], code_sems.at[line]
+        )
+
     code_copies = []
-    for slot in range(feat_slots):
-        for side in range(2):
-            line = 2 * slot + side
-            copy = pltpu.make_async_copy(
-                codes_hbm.at[pl.ds(pairs[side, first_pair + slot], 1)], codes.at[pl.ds(line, 1)], code_sems.at[line]
-            )
-            copy.start()
-            code_copies.append(copy)
+    for line in range(2 * feat_slots):
+        copy = code_copy(pairs[line % 2, first_pair + line // 2], line)
+        copy.start()
+        code_copies.append(copy)
     sums[...] = jnp.zeros_like(sums)
     half = BINS // 2
     levels = lax.broadcasted_iota(jnp.int32, (half, 1), 0).astype(jnp.float32)
     level_parts = (levels.astype(jnp.bfloat16), (levels + half).astype(jnp.bfloat16))
     grad_copy.wait()
     hess_copy.wait()
-    for narrow, wide in ((grad, grad_wide), (hess, hess_wide)):
-        values = narrow[...].astype(jnp.float32)
+    for flat, tall in ((grad, grad_tall), (hess, hess_tall)):
+        values = flat[...].astype(jnp.float32)
         for tile in range(row_count // LANES):
-            line = jnp.broadcast_to(values[tile : tile + 1], (half, LANES))
-            wide[:, tile * LANES : (tile + 1) * LANES] = line.astype(jnp.bfloat16)
+            square = jnp.broadcast_to(values[tile : tile + 1], (LANES, LANES)).astype(jnp.bfloat16)
+            tall[tile * LANES : (tile + 1) * LANES, :] = square.T
     zero = jnp.zeros((half, CHUNK), jnp.bfloat16)
     one = jnp.ones((half, CHUNK), jnp.bfloat16)
+
+    def below(line, span):
+        values = codes[pl.ds(line, 1), span].astype(jnp.float32)
+        values = jnp.broadcast_to(values, (half, CHUNK)).astype(jnp.bfloat16)
+        return [jnp.where(values <= level, one, zero) for level in level_parts]
+
     for copy in code_copies:
         copy.wait()
 
-    def spread(line, span):
-        values = codes[pl.ds(line, 1), span].astype(jnp.float32)
-        return jnp.broadcast_to(values, (half, CHUNK)).astype(jnp.bfloat16)
-
-    def step(index, carry):
-        span = pl.ds(pl.multiple_of(index * CHUNK, CHUNK), CHUNK)
-        grad_part = grad_wide[:, span]
-        hess_part = hess_wide[:, span]
+    def step(chunk, carry):
+        span = pl.ds(pl.multiple_of(chunk * CHUNK, CHUNK), CHUNK)
+        grad_part = grad_tall[span, :]
+        hess_part = hess_tall[span, :]
         for group in range(groups):
-            grad_rows, hess_rows, second_rows = [], [], []
+            first_rows, second_rows = [], []
             for pair in range(GROUP):
                 line = 2 * (GROUP * group + pair)
-                first = spread(line, span)
-                second = spread(line + 1, span)
-                for level in level_parts:
-                    below = first <= level
-                    grad_rows.append(jnp.where(below, grad_part, zero))
-                    hess_rows.append(jnp.where(below, hess_part, zero))
-                    second_rows.append(jnp.where(second <= level, one, zero))
-            weighted = jnp.concatenate(grad_rows + hess_rows, axis=0)
-            hot = jnp.concatenate(second_rows, axis=0)
-            sums[group] += lax.dot_general(
-                weighted, hot, (((1,), (1,)), ((), ())), preferred_element_type=jnp.float32
-            )
+                first_rows += below(line, span)
+                second_rows += below(line + 1, span)
+            first = jnp.concatenate(first_rows, axis=0)
+            second = jnp.concatenate(second_rows, axis=0).T
+            weighted = jnp.concatenate([second * grad_part, second * hess_part], axis=1)
+            sums[group] += jnp.dot(first, weighted, preferred_element_type=jnp.float32)
         return carry
 
-    lax.fori_loop(0, row_count // CHUNK, step, 0)
+    lax.fori_loop(0, chunks, step, 0)
     lane = lax.broadcasted_iota(jnp.int32, (BINS, LANES), 1)
     low = lane < LANES // 2
 
     def own_blocks(group, start):
-        block = sums[group, start : start + BINS]
+        block = sums[group, :BINS, start : start + LANES]
         for pair in range(1, GROUP):
-            at = start + pair * BINS
-            block = jnp.where(lane >= pair * BINS, sums[group, at : at + BINS], block)
+            at = pair * BINS
+            block = jnp.where(lane >= at, sums[group, at : at + BINS, start : start + LANES], block)
         return block
 
     for group in range(groups):
         grad_cum = own_blocks(group, 0)
-        hess_cum = own_blocks(group, GROUP * BINS)
+        hess_cum = own_blocks(group, LANES)
         out_ref[2 * group] = jnp.where(low, grad_cum, pltpu.roll(hess_cum, LANES // 2, 1))
         out_ref[2 * group + 1] = jnp.where(low, pltpu.roll(grad_cum, LANES // 2, 1), hess_cum)
     for message in range(2 * groups, out_ref.shape[0]):
@@ -116,9 +115,9 @@
             pltpu.VMEM((2 * feat_slots, row_count), jnp.int32),
             pltpu.VMEM((tiles, LANES), jnp.bfloat16),
             pltpu.VMEM((tiles, LANES), jnp.bfloat16),
-            pltpu.VMEM((BINS // 2, row_count), jnp.bfloat16),
-            pltpu.VMEM((BINS // 2, row_count), jnp.bfloat16),
-            pltpu.VMEM((groups, 2 * GROUP * BINS, GROUP * BINS), jnp.float32),
+            pltpu.VMEM((row_count, LANES), jnp.bfloat16),
+            pltpu.VMEM((row_count, LANES), jnp.bfloat16),
+            pltpu.VMEM((groups, GROUP * BINS, 2 * GROUP * BINS), jnp.float32),
             pltpu.SemaphoreType.DMA((2 * feat_slots,)),
             pltpu.SemaphoreType.DMA((3,)),
         ],

time: 34.1 us -> 31.8 us (0.933)
  Pallas kernels: 9.06 us -> 6.88 us
    pallas_call x1, Pallas kernels: 7.46 us -> 5.29 us  [cut_sums(): pl.pallas_call(functools.partial(cut_sums_kernel, feat_slots), out_shape=...]
where the time goes in v3:
time: 31.8 us; the launch traced here: 31.6 us
  blocking collectives  24 us (75%)
  Pallas kernels  6.88 us (22%)
  between operations  0.66 us (2%)
    all_to_all x1, blocking collectives, shards(): lax.all_to_all(partial, 'row', split_axis=0, concat_axis=0, tiled=True)  14.4 us
    all_to_all x1, blocking collectives, shards(): lax.all_to_all(outgoing, ('row', 'feat'), split_axis=0, concat_axis=0, ti...  9.62 us
    pallas_call x1, Pallas kernels, cut_sums(): pl.pallas_call(functools.partial(cut_sums_kernel, feat_slots), out_shape=...  5.29 us
    pallas_call x1, Pallas kernels, shards(): pl.pallas_call(functools.partial(table_kernel, feat_slots, feat_count), o...  1.31 us

profile of v3, /device:TPU:0, one launch (start us, length us, event | category | flops | bytes accessed | tf_op | source)
XLA Modules:
  0.0 31.6 jit_solution(18410194536297987769)
XLA Ops:
  0.6 0.0 copy-start
  0.6 5.3 %shard_map.68 = f32[8,32,128]{2,1,0:T(8,128)S(1)} custom-call(s32[2,64]{1,0:T(2,128)} %bitcast.8, s32[256,8192]{1,0:T(8,128)} %codes_hbm.1, bf16[64,128]{1,0:T(8,128)(2,1)} %bitcast.6, bf16[64,128]{1,0:T(8,128)(2,1)} %bitcast.7), custom_call_target="tpu_custom_call" | custom-call | tf_op jit(solution)/shard_map/pallas_call | solution.py:108
  5.9 14.4 %all_to_all.10.parts_ref = f32[8,32,128]{2,1,0:T(8,128)S(1)} all-to-all(f32[8,32,128]{2,1,0:T(8,128)S(1)} %shard_map.68), channel_id=1, replica_groups=mesh['row'=8,'feat'=4] {'row'}, dimensions={0} | all-to-all | bytes 262144 | tf_op jit(solution)/shard_map/all_to_all | solution.py:208
  20.3 0.3 shard_map.69
  20.6 9.6 %all_to_all.11.parts_ref = f32[32,4,128]{2,1,0:T(4,128)S(1)} all-to-all(f32[32,4,128]{2,1,0:T(4,128)S(1)} %bitcast.5), channel_id=1, replica_groups=mesh['row'=8,'feat'=4] {'row','feat'}, dimensions={0} | all-to-all | bytes 131072 | tf_op jit(solution)/shard_map/all_to_all | solution.py:218
  30.2 0.0 copy-done
  30.2 1.3 %shard_map.70 = (f32[32,128]{1,0:T(8,128)}, f32[1,64]{1,0:T(1,128)}) custom-call(s32[64]{0:T(128)S(1)} %copy-done, f32[32,4,128]{2,1,0:T(4,128)S(1)} %all_to_all.11.parts_ref), custom_call_target="tpu_custom_call" | custom-call | tf_op jit(solution)/shard_map/pallas_call | solution.py:219
Async XLA Ops:
  0.6 29.6 %copy-start = (s32[64]{0:T(128)S(1)}, s32[64]{0:T(128)}, u32[]{:S(2)}) copy-start(s32[64]{0:T(128)} %owners_ref.1) | copy-start | bytes 772

commit v4 on v3

--- a/solution.py
+++ b/solution.py
@@ -18,35 +18,61 @@
 SMALL_VMEM = 4 * 2**20
 
 
-def cut_sums_kernel(feat_slots, pairs_hbm, codes_hbm, grad_hbm, hess_hbm, out_ref, pairs, codes, grad, hess, grad_tall, hess_tall, sums, code_sems, small_sems):
+def route_tables(feat_slots, lines, pair_count):
+    feat_count = pair_count // feat_slots
+    row = lax.broadcasted_iota(jnp.int32, (pair_count, lines), 1)
+    source, part = row // PARTS, row % PARTS
+    place = source // feat_count * PER_MESSAGE + part
+    pair = source % feat_count * feat_slots + place
+    held = (part < PER_MESSAGE) & (place < feat_slots)
+    holders = held & (pair == lax.broadcasted_iota(jnp.int32, (pair_count, lines), 0))
+    square = (pair_count, pair_count)
+    earlier = lax.broadcasted_iota(jnp.int32, square, 0) < lax.broadcasted_iota(jnp.int32, square, 1)
+    return holders.astype(jnp.float32), earlier.astype(jnp.float32)
+
+
+def route(mine, holders, earlier, home_slots, shape):
+    owned = jnp.broadcast_to(mine.astype(jnp.float32), (8, mine.shape[1]))
+    rank = jnp.dot(owned, earlier, preferred_element_type=jnp.float32)
+    upper = lax.broadcasted_iota(jnp.int32, owned.shape, 0) == 0
+    spread = jnp.dot(jnp.where(upper, owned, rank), holders, preferred_element_type=jnp.float32)
+    slot = lax.broadcasted_iota(jnp.int32, shape, 0)
+    taken = jnp.where(spread[1:2].astype(jnp.int32) == slot, spread[0:1], 0.0)
+    best_row = jnp.where(lax.broadcasted_iota(jnp.int32, shape, 1) % PARTS == PER_MESSAGE, 1.0, 0.0)
+    return jnp.where(slot < home_slots, taken, best_row)
+
+
+def cut_sums_kernel(
+    feat_slots, home_slots, pairs_hbm, codes_hbm, grad_hbm, hess_hbm, owners_hbm, out_ref, route_ref,
+    pairs, codes, grad, hess, owners, grad_tall, hess_tall, sums, code_sem, small_sems,
+):
     groups = feat_slots // GROUP
-    first_pair = lax.axis_index("feat") * feat_slots
+    feat_index = lax.axis_index("feat")
+    first_pair = feat_index * feat_slots
     row_count = codes.shape[1]
     chunks = row_count // CHUNK
     pairs_copy = pltpu.make_async_copy(pairs_hbm, pairs, small_sems.at[0])
     grad_copy = pltpu.make_async_copy(grad_hbm, grad, small_sems.at[1])
     hess_copy = pltpu.make_async_copy(hess_hbm, hess, small_sems.at[2])
+    owners_copy = pltpu.make_async_copy(owners_hbm, owners, small_sems.at[3])
     pairs_copy.start()
     grad_copy.start()
     hess_copy.start()
+    owners_copy.start()
+    sums[...] = jnp.zeros_like(sums)
+    holders, earlier = route_tables(feat_slots, route_ref.shape[1], owners.shape[1])
     pairs_copy.wait()
 
-    def code_copy(feature, line):
-        return pltpu.make_async_copy(
-            codes_hbm.at[pl.ds(feature, 1)], codes.at[pl.ds(line, 1)], code_sems.at[line]
-        )
-
-    code_copies = []
     for line in range(2 * feat_slots):
-        copy = code_copy(pairs[line % 2, first_pair + line // 2], line)
-        copy.start()
-        code_copies.append(copy)
-    sums[...] = jnp.zeros_like(sums)
+        feature = pairs[line % 2, first_pair + line // 2]
+        pltpu.make_async_copy(codes_hbm.at[pl.ds(feature, 1)], codes.at[pl.ds(line, 1)], code_sem).start()
     half = BINS // 2
     levels = lax.broadcasted_iota(jnp.int32, (half, 1), 0).astype(jnp.float32)
     level_parts = (levels.astype(jnp.bfloat16), (levels + half).astype(jnp.bfloat16))
     grad_copy.wait()
     hess_copy.wait()
+    owners_copy.wait()
+    route_ref[...] = route(owners[...] == feat_index, holders, earlier, home_slots, route_ref.shape)
     for flat, tall in ((grad, grad_tall), (hess, hess_tall)):
         values = flat[...].astype(jnp.float32)
         for tile in range(row_count // LANES):
@@ -60,8 +86,7 @@
         values = jnp.broadcast_to(values, (half, CHUNK)).astype(jnp.bfloat16)
         return [jnp.where(values <= level, one, zero) for level in level_parts]
 
-    for copy in code_copies:
-        copy.wait()
+    pltpu.make_async_copy(codes_hbm.at[pl.ds(0, 2 * feat_slots)], codes, code_sem).wait()
 
     def step(chunk, carry):
         span = pl.ds(pl.multiple_of(chunk * CHUNK, CHUNK), CHUNK)
@@ -99,27 +124,36 @@
         out_ref[message] = jnp.zeros((BINS, LANES), jnp.float32)
 
 
-def cut_sums(bin_codes, gradients, hessians, pair_list, feat_slots, messages):
+def cut_sums(bin_codes, gradients, hessians, pair_list, owners, feat_slots, messages):
     row_count = bin_codes.shape[1]
     groups = feat_slots // GROUP
     tiles = row_count // LANES
+    pair_count = owners.shape[0]
+    feat_count = pair_count // feat_slots
+    home_slots = 2 * feat_slots
     anywhere = pl.BlockSpec(memory_space=pl.ANY)
-    operands = (pair_list.T, bin_codes, gradients.reshape(tiles, LANES), hessians.reshape(tiles, LANES))
+    in_vmem = pl.BlockSpec(memory_space=pltpu.VMEM)
+    flat = (gradients.reshape(tiles, LANES), hessians.reshape(tiles, LANES), owners.reshape(1, pair_count))
+    operands = (pair_list.T, bin_codes) + flat
     return pl.pallas_call(
-        functools.partial(cut_sums_kernel, feat_slots),
-        out_shape=jax.ShapeDtypeStruct((messages, BINS, LANES), jnp.float32),
-        in_specs=[anywhere] * 4,
-        out_specs=pl.BlockSpec(memory_space=pltpu.VMEM),
+        functools.partial(cut_sums_kernel, feat_slots, home_slots),
+        out_shape=(
+            jax.ShapeDtypeStruct((messages, BINS, LANES), jnp.float32),
+            jax.ShapeDtypeStruct((home_slots + 8, messages * feat_count * PARTS), jnp.float32),
+        ),
+        in_specs=[anywhere] * 5,
+        out_specs=(in_vmem, in_vmem),
         scratch_shapes=[
-            pltpu.SMEM((2, pair_list.shape[0]), jnp.int32),
+            pltpu.SMEM((2, pair_count), jnp.int32),
             pltpu.VMEM((2 * feat_slots, row_count), jnp.int32),
             pltpu.VMEM((tiles, LANES), jnp.bfloat16),
             pltpu.VMEM((tiles, LANES), jnp.bfloat16),
+            pltpu.VMEM((1, pair_count), jnp.int32),
             pltpu.VMEM((row_count, LANES), jnp.bfloat16),
             pltpu.VMEM((row_count, LANES), jnp.bfloat16),
             pltpu.VMEM((groups, GROUP * BINS, 2 * GROUP * BINS), jnp.float32),
-            pltpu.SemaphoreType.DMA((2 * feat_slots,)),
-            pltpu.SemaphoreType.DMA((3,)),
+            pltpu.SemaphoreType.DMA,
+            pltpu.SemaphoreType.DMA((4,)),
         ],
         compiler_params=pltpu.CompilerParams(vmem_limit_bytes=SUMS_VMEM),
     )(*(pltpu.with_memory_space_constraint(operand, pltpu.HBM) for operand in operands))
@@ -179,21 +213,25 @@
             out_ref[row, feat] = message
 
 
-def table_kernel(feat_slots, feat_count, owners_ref, parts_ref, table_ref, best_ref, table):
-    feat_index = lax.axis_index("feat")
-    home_slots, width = table_ref.shape
-    table[...] = jnp.zeros_like(table)
-    taken = jnp.int32(0)
-    for pair in range(owners_ref.shape[0]):
-        place = pair % feat_slots
-        source = place // PER_MESSAGE * feat_count + pair // feat_slots
-        mine = owners_ref[pair] == feat_index
-        slot = jnp.where(mine, jnp.minimum(taken, home_slots), home_slots)
-        table[pl.ds(slot, 1), :] = parts_ref[source, place % PER_MESSAGE : place % PER_MESSAGE + 1, :]
-        taken = taken + mine.astype(jnp.int32)
-    table_ref[...] = table[:home_slots, :width]
-    best = jnp.sum(parts_ref[:, PER_MESSAGE, :], axis=0, keepdims=True)
-    best_ref[...] = best[:, : best_ref.shape[1]]
+def table_kernel(route_ref, parts_ref, table_hbm, best_hbm, table, best, sems):
+    ways = route_ref[...].astype(jnp.bfloat16)
+    rest = parts_ref[...]
+    placed = jnp.zeros(route_ref.shape[:1] + rest.shape[1:], jnp.float32)
+    for _ in range(3):
+        part = rest.astype(jnp.bfloat16)
+        rest = rest - part.astype(jnp.float32)
+        placed = placed + jnp.dot(ways, part, preferred_element_type=jnp.float32)
+    home_slots, width = table.shape
+    table[...] = placed[:home_slots, :width]
+    best[...] = placed[home_slots : home_slots + 1, : best.shape[1]]
+    copies = (
+        pltpu.make_async_copy(table, table_hbm, sems.at[0]),
+        pltpu.make_async_copy(best, best_hbm, sems.at[1]),
+    )
+    for copy in copies:
+        copy.start()
+    for copy in copies:
+        copy.wait()
 
 
 def shards(bin_codes, gradients, hessians, pair_list, owners):
@@ -204,7 +242,7 @@
     home_slots = 2 * pair_count // feat_count
     width = BINS // row_count * BINS
     in_vmem = pl.BlockSpec(memory_space=pltpu.VMEM)
-    partial = cut_sums(bin_codes, gradients, hessians, pair_list, feat_slots, row_count)
+    partial, ways = cut_sums(bin_codes, gradients, hessians, pair_list, owners, feat_slots, row_count)
     parts = lax.all_to_all(partial, "row", split_axis=0, concat_axis=0, tiled=True)
     outgoing = pl.pallas_call(
         functools.partial(gains_kernel, feat_slots),
@@ -216,17 +254,23 @@
     )(parts)
     outgoing = outgoing.reshape(row_count * feat_count, PARTS, LANES)
     incoming = lax.all_to_all(outgoing, ("row", "feat"), split_axis=0, concat_axis=0, tiled=True)
+    incoming = incoming.reshape(row_count * feat_count * PARTS, LANES)
+    anywhere = pl.BlockSpec(memory_space=pl.ANY)
     cut_table, best = pl.pallas_call(
-        functools.partial(table_kernel, feat_slots, feat_count),
+        table_kernel,
         out_shape=(
             jax.ShapeDtypeStruct((home_slots, width), jnp.float32),
             jax.ShapeDtypeStruct((1, pair_count), jnp.float32),
         ),
-        in_specs=[pl.BlockSpec(memory_space=pltpu.SMEM), in_vmem],
-        out_specs=(in_vmem, in_vmem),
-        scratch_shapes=[pltpu.VMEM((home_slots + 8, LANES), jnp.float32)],
+        in_specs=[in_vmem, in_vmem],
+        out_specs=(anywhere, anywhere),
+        scratch_shapes=[
+            pltpu.VMEM((home_slots, width), jnp.float32),
+            pltpu.VMEM((1, pair_count), jnp.float32),
+            pltpu.SemaphoreType.DMA((2,)),
+        ],
         compiler_params=pltpu.CompilerParams(vmem_limit_bytes=SMALL_VMEM),
-    )(owners, incoming)
+    )(ways, incoming)
     return (cut_table, best.reshape(pair_count))
 
 

time: 31.8 us -> 30.8 us (0.969)
  Pallas kernels: 6.88 us -> 5.91 us
    pallas_call x2, Pallas kernels: 6.6 us -> 5.63 us  [the longest x1 4.84 us: cut_sums(): pl.pallas_call(functools.partial(cut_sums_kernel, feat_slots, home_slots)...]
where the time goes in v4:
time: 30.8 us; the launch traced here: 30.6 us
  blocking collectives  24 us (78%)
  Pallas kernels  5.91 us (19%)
  between operations  0.65 us (2%)
    all_to_all x1, blocking collectives, shards(): lax.all_to_all(partial, 'row', split_axis=0, concat_axis=0, tiled=True)  14.4 us
    all_to_all x1, blocking collectives, shards(): lax.all_to_all(outgoing, ('row', 'feat'), split_axis=0, concat_axis=0, ti...  9.63 us
    pallas_call x1, Pallas kernels, cut_sums(): pl.pallas_call(functools.partial(cut_sums_kernel, feat_slots, home_slots)...  4.84 us
    pallas_call x1, Pallas kernels, shards(): pl.pallas_call(table_kernel, out_shape=(jax.ShapeDtypeStruct((home_slots,...  0.79 us

profile of v4, /device:TPU:0, one launch (start us, length us, event | category | flops | bytes accessed | tf_op | source)
XLA Modules:
  0.0 30.6 jit_solution(882179041705684439)
XLA Ops:
  0.6 4.8 %shard_map.68 = (f32[8,32,128]{2,1,0:T(8,128)S(1)}, f32[40,128]{1,0:T(8,128)S(1)}) custom-call(s32[2,64]{1,0:T(2,128)} %bitcast.11, s32[256,8192]{1,0:T(8,128)} %codes_hbm.1, bf16[64,128]{1,0:T(8,128)(2,1)} %bitcast.9, bf16[64,128]{1,0:T(8,128)(2,1)} %bitcast.10, s32[1,64]{1,0:T(1,128)} %bitcast.12), custom_call_target="tpu_custom_call" | custom-call | tf_op jit(solution)/shard_map/pallas_call | solution.py:138
  5.5 14.4 %all_to_all.10.parts_ref = f32[8,32,128]{2,1,0:T(8,128)S(1)} all-to-all(f32[8,32,128]{2,1,0:T(8,128)S(1)} %get-tuple-element.7), channel_id=1, replica_groups=mesh['row'=8,'feat'=4] {'row'}, dimensions={0} | all-to-all | bytes 262144 | tf_op jit(solution)/shard_map/all_to_all | solution.py:246
  19.9 0.3 shard_map.69
  20.2 9.6 %all_to_all.11 = f32[32,4,128]{2,1,0:T(4,128)S(1)} all-to-all(f32[32,4,128]{2,1,0:T(4,128)S(1)} %bitcast.7), channel_id=1, replica_groups=mesh['row'=8,'feat'=4] {'row','feat'}, dimensions={0} | all-to-all | bytes 131072 | tf_op jit(solution)/shard_map/all_to_all | solution.py:256
  29.8 0.8 %shard_map.70 = (f32[32,128]{1,0:T(8,128)}, f32[1,64]{1,0:T(1,128)}) custom-call(f32[40,128]{1,0:T(8,128)S(1)} %get-tuple-element.6.route_ref, f32[128,128]{1,0:T(8,128)S(1)} %bitcast.8), custom_call_target="tpu_custom_call" | custom-call | tf_op jit(solution)/shard_map/pallas_call | solution.py:259

commit v5 on v4

v5 whole, which is shorter than its diff:
```python
import functools

import jax
import jax.numpy as jnp
from jax import lax
from jax.experimental import pallas as pl
from jax.experimental.pallas import tpu as pltpu
from jax.sharding import PartitionSpec as P

BINS = 32
LAMBDA_REG = 1.0
LANES = 128
CORES = 2
GROUP = 4
HALF = BINS // 2
PARTS = 4
CHUNK = 4096
HEAD = 5
LATE_HEAD = 5
SUMS_VMEM = 40 * 2**20
SMALL_VMEM = 4 * 2**20


class Plan:
    def __init__(self, row_count, feat_count, pair_count):
        self.row_count = row_count
        self.pair_count = pair_count
        self.chips = feat_count // CORES
        self.chip_pairs = pair_count // self.chips
        self.home_slots = 2 * pair_count // feat_count
        light = self.chip_pairs // GROUP // 4 * GROUP
        self.start = (0, light)
        self.count = (light, self.chip_pairs - light)
        self.per = tuple(-(-count // row_count) for count in self.count)
        self.head = HEAD * row_count // 8
        self.rows = [self.head] + [row for row in range(row_count) if row != self.head]
        self.members = row_count * self.chips
        self.late_head = LATE_HEAD * row_count // 8 * self.chips + self.chips - 1
        self.order = [self.late_head] + [member for member in range(self.members) if member != self.late_head]


def seat(member, head):
    return jnp.where(member == head, 0, jnp.where(member < head, member + 1, member))


def sitter(place, head):
    return jnp.where(place == 0, head, jnp.where(place <= head, place - 1, place))


def route_tables(plan):
    shape = (plan.pair_count, CORES * plan.members * PARTS)
    spot = lax.broadcasted_iota(jnp.int32, shape, 1)
    part, seated, other = spot % PARTS, spot // PARTS % plan.members, spot // (PARTS * plan.members)
    device = sitter(seated, plan.late_head)
    light = (lax.axis_index("feat") + other) % CORES == 0
    per, start, count = (jnp.where(light, values[0], values[1]) for values in (plan.per, plan.start, plan.count))
    place = seat(device // plan.chips, plan.head) * per + part
    pair = device % plan.chips * plan.chip_pairs + start + place
    held = (part < per) & (place < count)
    holders = held & (pair == lax.broadcasted_iota(jnp.int32, shape, 0))
    square = (plan.pair_count, plan.pair_count)
    earlier = lax.broadcasted_iota(jnp.int32, square, 0) < lax.broadcasted_iota(jnp.int32, square, 1)
    return holders.astype(jnp.float32), earlier.astype(jnp.float32)


def route(mine, holders, earlier, home_slots, shape):
    owned = jnp.broadcast_to(mine.astype(jnp.float32), (8, mine.shape[1]))
    rank = jnp.dot(owned, earlier, preferred_element_type=jnp.float32)
    upper = lax.broadcasted_iota(jnp.int32, owned.shape, 0) == 0
    spread = jnp.dot(jnp.where(upper, owned, rank), holders, preferred_element_type=jnp.float32)
    slot = lax.broadcasted_iota(jnp.int32, shape, 0)
    taken = jnp.where(spread[1:2].astype(jnp.int32) == slot, spread[0:1], 0.0)
    best_row = jnp.where(lax.broadcasted_iota(jnp.int32, shape, 1) % PARTS == PARTS - 1, 1.0, 0.0)
    return jnp.where(slot < home_slots, taken, best_row)


def cut_sums_kernel(
    plan, start, count, per, pairs_hbm, codes_hbm, grad_hbm, hess_hbm, owners_hbm, out_ref, route_ref,
    pairs, codes, grad, hess, owners, grad_tall, hess_tall, sums, code_sem, small_sems,
):
    groups = count // GROUP
    row_messages = out_ref.shape[0]
    feat_index = lax.axis_index("feat")
    first_pair = feat_index // CORES * plan.chip_pairs + start
    row_count = codes.shape[1]
    chunks = row_count // CHUNK
    pairs_copy = pltpu.make_async_copy(pairs_hbm, pairs, small_sems.at[0])
    grad_copy = pltpu.make_async_copy(grad_hbm, grad, small_sems.at[1])
    hess_copy = pltpu.make_async_copy(hess_hbm, hess, small_sems.at[2])
    owners_copy = pltpu.make_async_copy(owners_hbm, owners, small_sems.at[3])
    pairs_copy.start()
    grad_copy.start()
    hess_copy.start()
    owners_copy.start()
    sums[...] = jnp.zeros_like(sums)
    holders, earlier = route_tables(plan)
    pairs_copy.wait()

    for line in range(2 * count):
        feature = pairs[line % 2, first_pair + line // 2]
        pltpu.make_async_copy(codes_hbm.at[pl.ds(feature, 1)], codes.at[pl.ds(line, 1)], code_sem).start()
    levels = lax.broadcasted_iota(jnp.int32, (HALF, 1), 0).astype(jnp.float32)
    level_parts = (levels.astype(jnp.bfloat16), (levels + HALF).astype(jnp.bfloat16))
    grad_copy.wait()
    hess_copy.wait()
    owners_copy.wait()
    route_ref[...] = route(owners[...] == feat_index, holders, earlier, plan.home_slots, route_ref.shape)
    for flat, tall in ((grad, grad_tall), (hess, hess_tall)):
        values = flat[...].astype(jnp.float32)
        for tile in range(row_count // LANES):
            square = jnp.broadcast_to(values[tile : tile + 1], (LANES, LANES)).astype(jnp.bfloat16)
            tall[tile * LANES : (tile + 1) * LANES, :] = square.T
    zero = jnp.zeros((HALF, CHUNK), jnp.bfloat16)
    one = jnp.ones((HALF, CHUNK), jnp.bfloat16)

    def below(line, span):
        values = codes[pl.ds(line, 1), span].astype(jnp.float32)
        values = jnp.broadcast_to(values, (HALF, CHUNK)).astype(jnp.bfloat16)
        return [jnp.where(values <= level, one, zero) for level in level_parts]

    pltpu.make_async_copy(codes_hbm.at[pl.ds(0, 2 * count)], codes, code_sem).wait()

    def step(chunk, carry):
        span = pl.ds(pl.multiple_of(chunk * CHUNK, CHUNK), CHUNK)
        grad_part = grad_tall[span, :]
        hess_part = hess_tall[span, :]
        for group in range(groups):
            first_rows, second_rows = [], []
            for pair in range(GROUP):
                line = 2 * (GROUP * group + pair)
                first_rows += below(line, span)
                second_rows += below(line + 1, span)
            first = jnp.concatenate(first_rows, axis=0)
            second = jnp.concatenate(second_rows, axis=0).T
            weighted = jnp.concatenate([second * grad_part, second * hess_part], axis=1)
            sums[group] += jnp.dot(first, weighted, preferred_element_type=jnp.float32)
        return carry

    lax.fori_loop(0, chunks, step, 0)
    lane = lax.broadcasted_iota(jnp.int32, (HALF, LANES), 1)
    for place in range(row_messages * per):
        message, at = place // per, place % per * HALF
        if place >= count:
            out_ref[message, at : at + HALF] = jnp.zeros((HALF, LANES), jnp.float32)
            continue
        group, pair = place // GROUP, place % GROUP
        block = None
        for quarter in range(4):
            top, left = pair * BINS + quarter // 2 * HALF, quarter % 2 * LANES
            piece = sums[group, top : top + HALF, left : left + LANES]
            moved = (quarter - pair) * BINS % LANES
            if moved:
                piece = pltpu.roll(piece, moved, 1)
            block = piece if block is None else jnp.where(lane >= quarter * BINS, piece, block)
        out_ref[message, at : at + HALF] = block


def cut_sums(plan, core, bin_codes, gradients, hessians, pair_list, owners):
    row_count = bin_codes.shape[1]
    start, count, per = plan.start[core], plan.count[core], plan.per[core]
    groups = count // GROUP
    tiles = row_count // LANES
    anywhere = pl.BlockSpec(memory_space=pl.ANY)
    in_vmem = pl.BlockSpec(memory_space=pltpu.VMEM)
    flat = (gradients.reshape(tiles, LANES), hessians.reshape(tiles, LANES), owners.reshape(1, plan.pair_count))
    operands = (pair_list.T, bin_codes) + flat
    return pl.pallas_call(
        functools.partial(cut_sums_kernel, plan, start, count, per),
        out_shape=(
            jax.ShapeDtypeStruct((plan.row_count, per * HALF, LANES), jnp.float32),
            jax.ShapeDtypeStruct((plan.home_slots + 8, CORES * plan.members * PARTS), jnp.float32),
        ),
        in_specs=[anywhere] * 5,
        out_specs=(in_vmem, in_vmem),
        scratch_shapes=[
            pltpu.SMEM((2, plan.pair_count), jnp.int32),
            pltpu.VMEM((2 * count, row_count), jnp.int32),
            pltpu.VMEM((tiles, LANES), jnp.bfloat16),
            pltpu.VMEM((tiles, LANES), jnp.bfloat16),
            pltpu.VMEM((1, plan.pair_count), jnp.int32),
            pltpu.VMEM((row_count, LANES), jnp.bfloat16),
            pltpu.VMEM((row_count, LANES), jnp.bfloat16),
            pltpu.VMEM((groups, GROUP * BINS, 2 * GROUP * BINS), jnp.float32),
            pltpu.SemaphoreType.DMA,
            pltpu.SemaphoreType.DMA((4,)),
        ],
        compiler_params=pltpu.CompilerParams(vmem_limit_bytes=SUMS_VMEM),
    )(*(pltpu.with_memory_space_constraint(operand, pltpu.HBM) for operand in operands))


def pair_gains(sums):
    upper = lax.broadcasted_iota(jnp.int32, sums.shape, 1) >= LANES // 2

    def margins(cum):
        end = jnp.where(upper, cum[:, 3 * BINS - 1 : 3 * BINS], cum[:, BINS - 1 : BINS])
        last = cum[HALF - 1 :]
        return cum, end, jnp.where(upper[:1], last, pltpu.roll(last, LANES // 2, 1)), last[:, 3 * BINS - 1 : 3 * BINS]

    grad_cum, grad_end, grad_col, grad_all = margins(sums)
    hess_cum, hess_end, hess_col, hess_all = margins(pltpu.roll(sums, LANES - BINS, 1))
    result = -(grad_all * grad_all) / (hess_all + LAMBDA_REG)
    for grad_part, hess_part in (
        (grad_cum, hess_cum),
        (grad_end - grad_cum, hess_end - hess_cum),
        (grad_col - grad_cum, hess_col - hess_cum),
        (grad_all - grad_end - grad_col + grad_cum, hess_all - hess_end - hess_col + hess_cum),
    ):
        result = result + grad_part * grad_part / (hess_part + LAMBDA_REG)
    return result


def gains_kernel(plan, start, count, per, parts_ref, out_ref, gains):
    share = BINS // plan.row_count
    lines = plan.row_count // 2
    total = parts_ref[0]
    for part in range(1, plan.row_count):
        total = total + parts_ref[part]
    place = per * seat(lax.axis_index("row"), plan.head)
    first_pair = lax.axis_index("feat") // CORES * plan.chip_pairs + start + place
    line = lax.broadcasted_iota(jnp.int32, (1, LANES), 1)
    wide = lax.broadcasted_iota(jnp.int32, (lines, LANES), 1)
    best = jnp.zeros((1, LANES), jnp.float32)
    cuts = []
    for pair in range(per):
        result = pair_gains(total[pair * HALF : (pair + 1) * HALF])
        gains[pair] = result
        peak = jnp.max(result, axis=0, keepdims=True)
        top = jnp.max(jnp.where(line % (2 * BINS) < BINS, peak, -jnp.inf), axis=1, keepdims=True)
        best = jnp.where((line == first_pair + pair) & (place + pair < count), top, best)
        halves = []
        for half in range(2):
            laid = None
            for step in range(share):
                rows = gains[pair, pl.ds(step, lines, stride=share), :] if share > 1 else result
                moved = (step - 2 * half) * BINS % LANES
                if moved:
                    rows = pltpu.roll(rows, moved, 1)
                laid = rows if laid is None else jnp.where(wide >= step * BINS, rows, laid)
            halves.append(laid)
        cuts.append(halves)
    spot = lax.broadcasted_iota(jnp.int32, (PARTS, LANES), 0)
    messages = []
    for row in range(plan.row_count):
        message = jnp.broadcast_to(best, (PARTS, LANES))
        for pair in range(per):
            at = row % lines
            message = jnp.where(spot == pair, cuts[pair][row // lines][at : at + 1], message)
        messages.append(message)
    for place, member in enumerate(plan.order):
        out_ref[place] = messages[member // plan.chips]


def table_kernel(route_ref, near_ref, far_ref, table_hbm, best_hbm, table, best, sems):
    ways = route_ref[...].astype(jnp.bfloat16)
    rest = jnp.concatenate([near_ref[...], far_ref[...]], axis=0)
    placed = jnp.zeros(route_ref.shape[:1] + rest.shape[1:], jnp.float32)
    for _ in range(3):
        part = rest.astype(jnp.bfloat16)
        rest = rest - part.astype(jnp.float32)
        placed = placed + jnp.dot(ways, part, preferred_element_type=jnp.float32)
    home_slots, width = table.shape
    table[...] = placed[:home_slots, :width]
    best[...] = placed[home_slots : home_slots + 1, : best.shape[1]]
    copies = (
        pltpu.make_async_copy(table, table_hbm, sems.at[0]),
        pltpu.make_async_copy(best, best_hbm, sems.at[1]),
    )
    for copy in copies:
        copy.start()
    for copy in copies:
        copy.wait()


def core_part(plan, core, *arguments):
    row_groups = [plan.rows]
    member_groups = [[member * CORES + side for member in plan.order] for side in range(CORES)]
    partial, ways = cut_sums(plan, core, *arguments)
    parts = lax.all_to_all(partial, "row", split_axis=0, concat_axis=0, tiled=True, axis_index_groups=row_groups)
    start, count, per = plan.start[core], plan.count[core], plan.per[core]
    in_vmem = pl.BlockSpec(memory_space=pltpu.VMEM)
    outgoing = pl.pallas_call(
        functools.partial(gains_kernel, plan, start, count, per),
        out_shape=jax.ShapeDtypeStruct((plan.members, PARTS, LANES), jnp.float32),
        in_specs=[in_vmem],
        out_specs=in_vmem,
        scratch_shapes=[pltpu.VMEM((per, HALF, LANES), jnp.float32)],
        compiler_params=pltpu.CompilerParams(vmem_limit_bytes=SMALL_VMEM),
    )(parts)
    near = lax.all_to_all(
        outgoing, ("row", "feat"), split_axis=0, concat_axis=0, tiled=True, axis_index_groups=member_groups
    )
    return near.reshape(plan.members * PARTS, LANES), ways


def shards(*arguments):
    feat_count = lax.axis_size("feat")
    plan = Plan(lax.axis_size("row"), feat_count, arguments[-1].shape[0])
    branches = [functools.partial(core_part, plan, core) for core in range(CORES)]
    near, ways = lax.cond(lax.axis_index("feat") % CORES == 0, *branches, *arguments)
    swap = [(feat, feat // CORES * CORES + (feat + 1) % CORES) for feat in range(feat_count)]
    far = lax.ppermute(near, "feat", swap)
    width = BINS // plan.row_count * BINS
    anywhere = pl.BlockSpec(memory_space=pl.ANY)
    cut_table, best = pl.pallas_call(
        table_kernel,
        out_shape=(
            jax.ShapeDtypeStruct((plan.home_slots, width), jnp.float32),
            jax.ShapeDtypeStruct((1, plan.pair_count), jnp.float32),
        ),
        in_specs=[pl.BlockSpec(memory_space=pltpu.VMEM)] * 3,
        out_specs=(anywhere, anywhere),
        scratch_shapes=[
            pltpu.VMEM((plan.home_slots, width), jnp.float32),
            pltpu.VMEM((1, plan.pair_count), jnp.float32),
            pltpu.SemaphoreType.DMA((2,)),
        ],
        compiler_params=pltpu.CompilerParams(vmem_limit_bytes=SMALL_VMEM),
    )(ways, near, far)
    return (cut_table, best.reshape(plan.pair_count))


def solution(mesh):
    in_specs = (P(None, "row"), P("row"), P("row"), P(), P())
    out_specs = (P("feat", "row"), P())
    return jax.shard_map(shards, mesh=mesh, in_specs=in_specs, out_specs=out_specs, check_vma=False)
```

time: 30.8 us -> 27.9 us (0.906)
  blocking collectives: 24 us -> 20.8 us
  Pallas kernels: 5.91 us -> 4.71 us
  waiting for transfers between devices: 0 us -> 0.86 us
  starting transfers between devices: 0 us -> 0.47 us
    all_to_all x2, blocking collectives: 24 us -> 20.8 us  [the longest x1 11.1 us: core_part(): lax.all_to_all(partial, 'row', split_axis=0, concat_axis=0, tiled=True, a...]
    pallas_call x3, Pallas kernels: 5.91 us -> 4.71 us  [the longest x1 3.64 us: cut_sums(): pl.pallas_call(functools.partial(cut_sums_kernel, plan, start, count, per...]
    ppermute x0 -> x1, waiting for transfers between devices: none -> 0.86 us  [shards(): far = lax.ppermute(near, 'feat', swap)]
    ppermute x0 -> x1, starting transfers between devices: none -> 0.47 us  [shards(): far = lax.ppermute(near, 'feat', swap)]
  transfers between devices with their start and end apart: 0 -> 1, of which waited for: 0 -> 1; matrix products, arithmetic and copies ran while one was open for 0% -> 0% of each run, Pallas kernels for 0% -> 0%
where the time goes in v5:
time: 27.9 us; the launch traced here: 27.6 us
  blocking collectives  20.8 us (75%)
  Pallas kernels  4.71 us (17%)
  waiting for transfers between devices  0.86 us (3%)
  between operations  0.64 us (2%)
  starting transfers between devices  0.47 us (2%)
    all_to_all x1, blocking collectives, core_part(): lax.all_to_all(partial, 'row', split_axis=0, concat_axis=0, tiled=True, a...  11.1 us
    all_to_all x1, blocking collectives, core_part(): lax.all_to_all(outgoing, ('row', 'feat'), split_axis=0, concat_axis=0, ti...  9.76 us
    pallas_call x1, Pallas kernels, cut_sums(): pl.pallas_call(functools.partial(cut_sums_kernel, plan, start, count, per...  3.64 us
    ppermute x1, waiting for transfers between devices, shards(): far = lax.ppermute(near, 'feat', swap)  0.86 us
    pallas_call x1, Pallas kernels, shards(): pl.pallas_call(table_kernel, out_shape=(jax.ShapeDtypeStruct((plan.home_s...  0.79 us
  transfers between devices with their start and end apart: 1, of which 1 were waited for; matrix products, arithmetic and copies ran while one was open for 0% of the time, Pallas kernels for 0%

profile of v5, /device:TPU:0, one launch (start us, length us, event | category | flops | bytes accessed | tf_op | source)
XLA Modules:
  0.0 27.6 jit_solution(5735143549397361900)
XLA Ops:
  0.6 24.8 %conditional.1 = (f32[40,128]{1,0:T(8,128)S(1)}, f32[64,128]{1,0:T(8,128)S(1)}) conditional(s32[]{:T(128)} %convert_element_type.3, (s32[64,2]{0,1:T(2,128)}, bf16[8192]{0:T(1024)(128)(2,1)}, bf16[8192]{0:T(1024)(128)(2,1)}, s32[64]{0:T(128)}, s32[256,8192]{1,0:T(8,128)}) %tuple.21, (s32[64,2]{0,1:T(2,128)}, bf16[8192]{0:T(1024)(128)(2,1)}, ...), branch_computations={%region_0.1_spmd, %region_1.2_spmd} | conditional | bytes 458768 | solution.py:299
  0.7 3.6 %branch_1_fun.2 = (f32[8,16,128]{2,1,0:T(8,128)S(1)}, f32[40,128]{1,0:T(8,128)S(1)}) custom-call(s32[2,64]{1,0:T(2,128)} %bitcast.18, s32[256,8192]{1,0:T(8,128)} %get-tuple-element.31.codes_hbm, bf16[64,128]{1,0:T(8,128)(2,1)} %bitcast.14, bf16[64,128]{1,0:T(8,128)(2,1)} %bitcast.16, s32[1,64]{1,0:T(1,128)} %bitcast.20), custom_call_target="tpu_custom_call" | custom-call | tf_op jit(solution)/shard_map/cond/branch_1_fun/pallas_call | solution.py:167
  4.3 11.1 %all_to_all.18.parts_ref = f32[8,16,128]{2,1,0:T(8,128)S(1)} all-to-all(f32[8,16,128]{2,1,0:T(8,128)S(1)} %get-tuple-element.36), channel_id=1, replica_groups={{20,0,4,8,12,16,24,28},{21,1,5,9,13,17,25,29},{22,2,6,10,14,18,26,30},{..., dimensions={0} | all-to-all | bytes 131072 | tf_op jit(solution)/shard_map/cond/branch_1_fun/all_to_all | solution.py:278
  15.4 0.3 %branch_1_fun.3 = f32[16,4,128]{2,1,0:T(4,128)S(1)} custom-call(f32[8,16,128]{2,1,0:T(8,128)S(1)} %all_to_all.18.parts_ref), custom_call_target="tpu_custom_call" | custom-call | tf_op jit(solution)/shard_map/cond/branch_1_fun/pallas_call | solution.py:281
  15.7 9.8 %all_to_all.19 = f32[16,4,128]{2,1,0:T(4,128)S(1)} all-to-all(f32[16,4,128]{2,1,0:T(4,128)S(1)} %branch_1_fun.3), channel_id=1, replica_groups={{22,0,2,4,6,8,10,12,14,16,18,20,24,26,28,30},{23,1,3,5,7,9,11,13,15,17,..., dimensions={0} | all-to-all | bytes 65536 | tf_op jit(solution)/shard_map/cond/branch_1_fun/all_to_all | solution.py:289
  25.4 0.5 %collective-permute-start = (f32[64,128]{1,0:T(8,128)S(1)}, f32[64,128]{1,0:T(8,128)S(1)}, u32[]{:S(2)}, u32[]{:S(2)}) collective-permute-start(f32[64,128]{1,0:T(8,128)S(1)} %get-tuple-element.49.near_ref), channel_id=1, source_target_pairs={{0,1},{1,0},{2,3},{3,2},{4,5},{5,4},{6,7},{7,6},{8,9},{9,8},{10,11... | collective-permute-start | bytes 98312 | tf_op jit(solution)/shard_map/ppermute | solution.py:301
  25.9 0.9 %collective-permute-done.far_ref = f32[64,128]{1,0:T(8,128)S(1)} collective-permute-done((f32[64,128]{1,0:T(8,128)S(1)}, f32[64,128]{1,0:T(8,128)S(1)}, u32[]{:S(2)}, u32[]{:S(2)}) %collective-permute-start) | collective-permute-done | bytes 32800 | tf_op jit(solution)/shard_map/ppermute | solution.py:301
  26.8 0.8 %shard_map.68 = (f32[32,128]{1,0:T(8,128)}, f32[1,64]{1,0:T(1,128)}) custom-call(f32[40,128]{1,0:T(8,128)S(1)} %get-tuple-element.47.route_ref, f32[64,128]{1,0:T(8,128)S(1)} %get-tuple-element.49.near_ref, f32[64,128]{1,0:T(8,128)S(1)} %collective-permute-done.far_ref), custom_call_target="tpu_custom_call" | custom-call | tf_op jit(solution)/shard_map/pallas_call | solution.py:304
Async XLA Ops:
  25.4 1.3 %collective-permute-start = (f32[64,128]{1,0:T(8,128)S(1)}, f32[64,128]{1,0:T(8,128)S(1)}, u32[]{:S(2)}, u32[]{:S(2)}) collective-permute-start(f32[64,128]{1,0:T(8,128)S(1)} %get-tuple-element.49.near_ref), channel_id=1, source_target_pairs={{0,1},{1,0},{2,3},{3,2},{4,5},{5,4},{6,7},{7,6},{8,9},{9,8},{10,11... | collective-permute-start | bytes 98312 | tf_op jit(solution)/shard_map/ppermute | solution.py:301

commit v6 on v5

--- a/solution.py
+++ b/solution.py
@@ -14,10 +14,10 @@
 GROUP = 4
 HALF = BINS // 2
 PARTS = 4
-CHUNK = 4096
+CHUNK = 2048
 HEAD = 5
 LATE_HEAD = 5
-SUMS_VMEM = 40 * 2**20
+SUMS_VMEM = 48 * 2**20
 SMALL_VMEM = 4 * 2**20
 
 
@@ -79,11 +79,10 @@
     pairs, codes, grad, hess, owners, grad_tall, hess_tall, sums, code_sem, small_sems,
 ):
     groups = count // GROUP
+    row_count = codes.shape[1]
     row_messages = out_ref.shape[0]
     feat_index = lax.axis_index("feat")
     first_pair = feat_index // CORES * plan.chip_pairs + start
-    row_count = codes.shape[1]
-    chunks = row_count // CHUNK
     pairs_copy = pltpu.make_async_copy(pairs_hbm, pairs, small_sems.at[0])
     grad_copy = pltpu.make_async_copy(grad_hbm, grad, small_sems.at[1])
     hess_copy = pltpu.make_async_copy(hess_hbm, hess, small_sems.at[2])
@@ -92,7 +91,6 @@
     grad_copy.start()
     hess_copy.start()
     owners_copy.start()
-    sums[...] = jnp.zeros_like(sums)
     holders, earlier = route_tables(plan)
     pairs_copy.wait()
 
@@ -114,17 +112,15 @@
     one = jnp.ones((HALF, CHUNK), jnp.bfloat16)
 
     def below(line, span):
-        values = codes[pl.ds(line, 1), span].astype(jnp.float32)
+        values = codes[line : line + 1, span].astype(jnp.float32)
         values = jnp.broadcast_to(values, (HALF, CHUNK)).astype(jnp.bfloat16)
         return [jnp.where(values <= level, one, zero) for level in level_parts]
 
     pltpu.make_async_copy(codes_hbm.at[pl.ds(0, 2 * count)], codes, code_sem).wait()
-
-    def step(chunk, carry):
-        span = pl.ds(pl.multiple_of(chunk * CHUNK, CHUNK), CHUNK)
-        grad_part = grad_tall[span, :]
-        hess_part = hess_tall[span, :]
-        for group in range(groups):
+    for group in range(groups):
+        total = None
+        for begin in range(0, row_count, CHUNK):
+            span = slice(begin, begin + CHUNK)
             first_rows, second_rows = [], []
             for pair in range(GROUP):
                 line = 2 * (GROUP * group + pair)
@@ -132,11 +128,10 @@
                 second_rows += below(line + 1, span)
             first = jnp.concatenate(first_rows, axis=0)
             second = jnp.concatenate(second_rows, axis=0).T
-            weighted = jnp.concatenate([second * grad_part, second * hess_part], axis=1)
-            sums[group] += jnp.dot(first, weighted, preferred_element_type=jnp.float32)
-        return carry
-
-    lax.fori_loop(0, chunks, step, 0)
+            weighted = jnp.concatenate([second * grad_tall[span, :], second * hess_tall[span, :]], axis=1)
+            product = jnp.dot(first, weighted, preferred_element_type=jnp.float32)
+            total = product if total is None else total + product
+        sums[group] = total
     lane = lax.broadcasted_iota(jnp.int32, (HALF, LANES), 1)
     for place in range(row_messages * per):
         message, at = place // per, place % per * HALF

time: 27.9 us -> 27.5 us (0.986)
    all_to_all x1, blocking collectives: 9.76 us -> 9.48 us  [core_part(): lax.all_to_all(outgoing, ('row', 'feat'), split_axis=0, concat_axis=0, ti...]
where the time goes in v6:
time: 27.5 us; the launch traced here: 27.1 us
  blocking collectives  20.7 us (75%)
  Pallas kernels  4.45 us (16%)
  waiting for transfers between devices  0.86 us (3%)
  between operations  0.64 us (2%)
  starting transfers between devices  0.44 us (2%)
    all_to_all x1, blocking collectives, core_part(): lax.all_to_all(partial, 'row', split_axis=0, concat_axis=0, tiled=True, a...  11.2 us
    all_to_all x1, blocking collectives, core_part(): lax.all_to_all(outgoing, ('row', 'feat'), split_axis=0, concat_axis=0, ti...  9.48 us
    pallas_call x1, Pallas kernels, cut_sums(): pl.pallas_call(functools.partial(cut_sums_kernel, plan, start, count, per...  3.39 us
    ppermute x1, waiting for transfers between devices, shards(): far = lax.ppermute(near, 'feat', swap)  0.86 us
    pallas_call x1, Pallas kernels, shards(): pl.pallas_call(table_kernel, out_shape=(jax.ShapeDtypeStruct((plan.home_s...  0.79 us
  transfers between devices with their start and end apart: 1, of which 1 were waited for; matrix products, arithmetic and copies ran while one was open for 0% of the time, Pallas kernels for 0%

profile of v6, /device:TPU:0, one launch (start us, length us, event | category | flops | bytes accessed | tf_op | source)
XLA Modules:
  0.0 27.1 jit_solution(15446135836661621741)
XLA Ops:
  0.6 24.4 %conditional.1 = (f32[40,128]{1,0:T(8,128)S(1)}, f32[64,128]{1,0:T(8,128)S(1)}) conditional(s32[]{:T(128)} %convert_element_type.3, (s32[64,2]{0,1:T(2,128)}, bf16[8192]{0:T(1024)(128)(2,1)}, bf16[8192]{0:T(1024)(128)(2,1)}, s32[64]{0:T(128)}, s32[256,8192]{1,0:T(8,128)}) %tuple.21, (s32[64,2]{0,1:T(2,128)}, bf16[8192]{0:T(1024)(128)(2,1)}, ...), branch_computations={%region_0.1_spmd, %region_1.2_spmd} | conditional | bytes 458768 | solution.py:294
  0.7 3.4 %branch_1_fun.2 = (f32[8,16,128]{2,1,0:T(8,128)S(1)}, f32[40,128]{1,0:T(8,128)S(1)}) custom-call(s32[2,64]{1,0:T(2,128)} %bitcast.18, s32[256,8192]{1,0:T(8,128)} %get-tuple-element.31.codes_hbm, bf16[64,128]{1,0:T(8,128)(2,1)} %bitcast.14, bf16[64,128]{1,0:T(8,128)(2,1)} %bitcast.16, s32[1,64]{1,0:T(1,128)} %bitcast.20), custom_call_target="tpu_custom_call" | custom-call | tf_op jit(solution)/shard_map/cond/branch_1_fun/pallas_call | solution.py:162
  4.1 11.2 %all_to_all.18.parts_ref = f32[8,16,128]{2,1,0:T(8,128)S(1)} all-to-all(f32[8,16,128]{2,1,0:T(8,128)S(1)} %get-tuple-element.36), channel_id=1, replica_groups={{20,0,4,8,12,16,24,28},{21,1,5,9,13,17,25,29},{22,2,6,10,14,18,26,30},{..., dimensions={0} | all-to-all | bytes 131072 | tf_op jit(solution)/shard_map/cond/branch_1_fun/all_to_all | solution.py:273
  15.3 0.3 %branch_1_fun.3 = f32[16,4,128]{2,1,0:T(4,128)S(1)} custom-call(f32[8,16,128]{2,1,0:T(8,128)S(1)} %all_to_all.18.parts_ref), custom_call_target="tpu_custom_call" | custom-call | tf_op jit(solution)/shard_map/cond/branch_1_fun/pallas_call | solution.py:276
  15.6 9.5 %all_to_all.19 = f32[16,4,128]{2,1,0:T(4,128)S(1)} all-to-all(f32[16,4,128]{2,1,0:T(4,128)S(1)} %branch_1_fun.3), channel_id=1, replica_groups={{22,0,2,4,6,8,10,12,14,16,18,20,24,26,28,30},{23,1,3,5,7,9,11,13,15,17,..., dimensions={0} | all-to-all | bytes 65536 | tf_op jit(solution)/shard_map/cond/branch_1_fun/all_to_all | solution.py:284
  25.0 0.4 %collective-permute-start = (f32[64,128]{1,0:T(8,128)S(1)}, f32[64,128]{1,0:T(8,128)S(1)}, u32[]{:S(2)}, u32[]{:S(2)}) collective-permute-start(f32[64,128]{1,0:T(8,128)S(1)} %get-tuple-element.49.near_ref), channel_id=1, source_target_pairs={{0,1},{1,0},{2,3},{3,2},{4,5},{5,4},{6,7},{7,6},{8,9},{9,8},{10,11... | collective-permute-start | bytes 98312 | tf_op jit(solution)/shard_map/ppermute | solution.py:296
  25.5 0.9 %collective-permute-done.far_ref = f32[64,128]{1,0:T(8,128)S(1)} collective-permute-done((f32[64,128]{1,0:T(8,128)S(1)}, f32[64,128]{1,0:T(8,128)S(1)}, u32[]{:S(2)}, u32[]{:S(2)}) %collective-permute-start) | collective-permute-done | bytes 32800 | tf_op jit(solution)/shard_map/ppermute | solution.py:296
  26.3 0.8 %shard_map.68 = (f32[32,128]{1,0:T(8,128)}, f32[1,64]{1,0:T(1,128)}) custom-call(f32[40,128]{1,0:T(8,128)S(1)} %get-tuple-element.47.route_ref, f32[64,128]{1,0:T(8,128)S(1)} %get-tuple-element.49.near_ref, f32[64,128]{1,0:T(8,128)S(1)} %collective-permute-done.far_ref), custom_call_target="tpu_custom_call" | custom-call | tf_op jit(solution)/shard_map/pallas_call | solution.py:299
Async XLA Ops:
  25.0 1.3 %collective-permute-start = (f32[64,128]{1,0:T(8,128)S(1)}, f32[64,128]{1,0:T(8,128)S(1)}, u32[]{:S(2)}, u32[]{:S(2)}) collective-permute-start(f32[64,128]{1,0:T(8,128)S(1)} %get-tuple-element.49.near_ref), channel_id=1, source_target_pairs={{0,1},{1,0},{2,3},{3,2},{4,5},{5,4},{6,7},{7,6},{8,9},{9,8},{10,11... | collective-permute-start | bytes 98312 | tf_op jit(solution)/shard_map/ppermute | solution.py:296

commit v7 on v6

--- a/solution.py
+++ b/solution.py
@@ -17,6 +17,8 @@
 CHUNK = 2048
 HEAD = 5
 LATE_HEAD = 5
+ROW_ORDERS = {8: [5, 1, 0, 2, 3, 7, 4, 6]}
+MEMBER_ORDERS = {16: [11, 10, 12, 5, 9, 0, 6, 3, 15, 8, 1, 14, 7, 2, 13, 4]}
 SUMS_VMEM = 48 * 2**20
 SMALL_VMEM = 4 * 2**20
 
@@ -32,29 +34,44 @@
         self.start = (0, light)
         self.count = (light, self.chip_pairs - light)
         self.per = tuple(-(-count // row_count) for count in self.count)
-        self.head = HEAD * row_count // 8
-        self.rows = [self.head] + [row for row in range(row_count) if row != self.head]
+        self.rows = group_order(row_count, HEAD * row_count // 8, ROW_ORDERS)
         self.members = row_count * self.chips
-        self.late_head = LATE_HEAD * row_count // 8 * self.chips + self.chips - 1
-        self.order = [self.late_head] + [member for member in range(self.members) if member != self.late_head]
-
-
-def seat(member, head):
-    return jnp.where(member == head, 0, jnp.where(member < head, member + 1, member))
-
-
-def sitter(place, head):
-    return jnp.where(place == 0, head, jnp.where(place <= head, place - 1, place))
+        late_head = LATE_HEAD * row_count // 8 * self.chips + self.chips - 1
+        self.order = group_order(self.members, late_head, MEMBER_ORDERS)
+
+
+def group_order(size, head, orders):
+    return orders.get(size, [head] + [member for member in range(size) if member != head])
+
+
+def seat(member, order):
+    head = order[0]
+    if order[1:] == sorted(order[1:]):
+        return jnp.where(member == head, 0, jnp.where(member < head, member + 1, member))
+    place = jnp.zeros_like(member)
+    for at, who in enumerate(order):
+        place = jnp.where(member == who, at, place)
+    return place
+
+
+def sitter(place, order):
+    head = order[0]
+    if order[1:] == sorted(order[1:]):
+        return jnp.where(place == 0, head, jnp.where(place <= head, place - 1, place))
+    member = jnp.zeros_like(place)
+    for at, who in enumerate(order):
+        member = jnp.where(place == at, who, member)
+    return member
 
 
 def route_tables(plan):
     shape = (plan.pair_count, CORES * plan.members * PARTS)
     spot = lax.broadcasted_iota(jnp.int32, shape, 1)
     part, seated, other = spot % PARTS, spot // PARTS % plan.members, spot // (PARTS * plan.members)
-    device = sitter(seated, plan.late_head)
+    device = sitter(seated, plan.order)
     light = (lax.axis_index("feat") + other) % CORES == 0
     per, start, count = (jnp.where(light, values[0], values[1]) for values in (plan.per, plan.start, plan.count))
-    place = seat(device // plan.chips, plan.head) * per + part
+    place = seat(device // plan.chips, plan.rows) * per + part
     pair = device % plan.chips * plan.chip_pairs + start + place
     held = (part < per) & (place < count)
     holders = held & (pair == lax.broadcasted_iota(jnp.int32, shape, 0))
@@ -210,7 +227,7 @@
     total = parts_ref[0]
     for part in range(1, plan.row_count):
         total = total + parts_ref[part]
-    place = per * seat(lax.axis_index("row"), plan.head)
+    place = per * seat(lax.axis_index("row"), plan.rows)
     first_pair = lax.axis_index("feat") // CORES * plan.chip_pairs + start + place
     line = lax.broadcasted_iota(jnp.int32, (1, LANES), 1)
     wide = lax.broadcasted_iota(jnp.int32, (lines, LANES), 1)
@@ -245,7 +262,7 @@
         out_ref[place] = messages[member // plan.chips]
 
 
-def table_kernel(route_ref, near_ref, far_ref, table_hbm, best_hbm, table, best, sems):
+def table_kernel(route_ref, near_ref, far_ref, table, best):
     ways = route_ref[...].astype(jnp.bfloat16)
     rest = jnp.concatenate([near_ref[...], far_ref[...]], axis=0)
     placed = jnp.zeros(route_ref.shape[:1] + rest.shape[1:], jnp.float32)
@@ -256,14 +273,6 @@
     home_slots, width = table.shape
     table[...] = placed[:home_slots, :width]
     best[...] = placed[home_slots : home_slots + 1, : best.shape[1]]
-    copies = (
-        pltpu.make_async_copy(table, table_hbm, sems.at[0]),
-        pltpu.make_async_copy(best, best_hbm, sems.at[1]),
-    )
-    for copy in copies:
-        copy.start()
-    for copy in copies:
-        copy.wait()
 
 
 def core_part(plan, core, *arguments):
@@ -295,7 +304,6 @@
     swap = [(feat, feat // CORES * CORES + (feat + 1) % CORES) for feat in range(feat_count)]
     far = lax.ppermute(near, "feat", swap)
     width = BINS // plan.row_count * BINS
-    anywhere = pl.BlockSpec(memory_space=pl.ANY)
     cut_table, best = pl.pallas_call(
         table_kernel,
         out_shape=(
@@ -303,12 +311,7 @@
             jax.ShapeDtypeStruct((1, plan.pair_count), jnp.float32),
         ),
         in_specs=[pl.BlockSpec(memory_space=pltpu.VMEM)] * 3,
-        out_specs=(anywhere, anywhere),
-        scratch_shapes=[
-            pltpu.VMEM((plan.home_slots, width), jnp.float32),
-            pltpu.VMEM((1, plan.pair_count), jnp.float32),
-            pltpu.SemaphoreType.DMA((2,)),
-        ],
+        out_specs=[pl.BlockSpec(memory_space=pltpu.VMEM)] * 2,
         compiler_params=pltpu.CompilerParams(vmem_limit_bytes=SMALL_VMEM),
     )(ways, near, far)
     return (cut_table, best.reshape(plan.pair_count))

time: 27.5 us -> 27.2 us (0.989)
  no operation moved by 1% of the time
where the time goes in v7:
time: 27.2 us; the launch traced here: 26.9 us
  blocking collectives  20.6 us (76%)
  Pallas kernels  4.43 us (16%)
  waiting for transfers between devices  0.97 us (4%)
  between operations  0.64 us (2%)
    all_to_all x1, blocking collectives, core_part(): lax.all_to_all(partial, 'row', split_axis=0, concat_axis=0, tiled=True, a...  11.3 us
    all_to_all x1, blocking collectives, core_part(): lax.all_to_all(outgoing, ('row', 'feat'), split_axis=0, concat_axis=0, ti...  9.29 us
    pallas_call x1, Pallas kernels, cut_sums(): pl.pallas_call(functools.partial(cut_sums_kernel, plan, start, count, per...  3.39 us
    ppermute x1, waiting for transfers between devices, shards(): far = lax.ppermute(near, 'feat', swap)  0.97 us
    pallas_call x1, Pallas kernels, shards(): pl.pallas_call(table_kernel, out_shape=(jax.ShapeDtypeStruct((plan.home_s...  0.77 us
  transfers between devices with their start and end apart: 1, of which 1 were waited for; matrix products, arithmetic and copies ran while one was open for 0% of the time, Pallas kernels for 0%

profile of v7, /device:TPU:0, one launch (start us, length us, event | category | flops | bytes accessed | tf_op | source)
XLA Modules:
  0.0 26.9 jit_solution(6165417396440341725)
XLA Ops:
  0.6 24.3 %conditional.1 = (f32[40,128]{1,0:T(8,128)S(1)}, f32[64,128]{1,0:T(8,128)S(1)}) conditional(s32[]{:T(128)} %convert_element_type.3, (s32[64,2]{0,1:T(2,128)}, bf16[8192]{0:T(1024)(128)(2,1)}, bf16[8192]{0:T(1024)(128)(2,1)}, s32[64]{0:T(128)}, s32[256,8192]{1,0:T(8,128)}) %tuple.21, (s32[64,2]{0,1:T(2,128)}, bf16[8192]{0:T(1024)(128)(2,1)}, ...), branch_computations={%region_0.1_spmd, %region_1.2_spmd} | conditional | bytes 458768 | solution.py:303
  0.7 3.4 %branch_1_fun.2 = (f32[8,16,128]{2,1,0:T(8,128)S(1)}, f32[40,128]{1,0:T(8,128)S(1)}) custom-call(s32[2,64]{1,0:T(2,128)} %bitcast.18, s32[256,8192]{1,0:T(8,128)} %get-tuple-element.31.codes_hbm, bf16[64,128]{1,0:T(8,128)(2,1)} %bitcast.14, bf16[64,128]{1,0:T(8,128)(2,1)} %bitcast.16, s32[1,64]{1,0:T(1,128)} %bitcast.20), custom_call_target="tpu_custom_call" | custom-call | tf_op jit(solution)/shard_map/cond/branch_1_fun/pallas_call | solution.py:179
  4.1 11.3 %all_to_all.18.parts_ref = f32[8,16,128]{2,1,0:T(8,128)S(1)} all-to-all(f32[8,16,128]{2,1,0:T(8,128)S(1)} %get-tuple-element.36), channel_id=1, replica_groups={{20,4,0,8,12,28,16,24},{21,5,1,9,13,29,17,25},{22,6,2,10,14,30,18,26},{..., dimensions={0} | all-to-all | bytes 131072 | tf_op jit(solution)/shard_map/cond/branch_1_fun/all_to_all | solution.py:282
  15.3 0.3 %branch_1_fun.3 = f32[16,4,128]{2,1,0:T(4,128)S(1)} custom-call(f32[8,16,128]{2,1,0:T(8,128)S(1)} %all_to_all.18.parts_ref), custom_call_target="tpu_custom_call" | custom-call | tf_op jit(solution)/shard_map/cond/branch_1_fun/pallas_call | solution.py:285
  15.6 9.3 %all_to_all.19 = f32[16,4,128]{2,1,0:T(4,128)S(1)} all-to-all(f32[16,4,128]{2,1,0:T(4,128)S(1)} %branch_1_fun.3), channel_id=1, replica_groups={{22,20,24,10,18,0,12,6,30,16,2,28,14,4,26,8},{23,21,25,11,19,1,13,7,31,..., dimensions={0} | all-to-all | bytes 65536 | tf_op jit(solution)/shard_map/cond/branch_1_fun/all_to_all | solution.py:293
  24.9 0.2 collective-permute-start
  25.2 1.0 %collective-permute-done.far_ref = f32[64,128]{1,0:T(8,128)S(1)} collective-permute-done((f32[64,128]{1,0:T(8,128)S(1)}, f32[64,128]{1,0:T(8,128)S(1)}, u32[]{:S(2)}, u32[]{:S(2)}) %collective-permute-start) | collective-permute-done | bytes 32800 | tf_op jit(solution)/shard_map/ppermute | solution.py:305
  26.1 0.8 %shard_map.68 = (f32[32,128]{1,0:T(8,128)}, f32[1,64]{1,0:T(1,128)}) custom-call(f32[40,128]{1,0:T(8,128)S(1)} %get-tuple-element.47.route_ref, f32[64,128]{1,0:T(8,128)S(1)} %get-tuple-element.49.near_ref, f32[64,128]{1,0:T(8,128)S(1)} %collective-permute-done.far_ref), custom_call_target="tpu_custom_call" | custom-call | tf_op jit(solution)/shard_map/pallas_call | solution.py:307
Async XLA Ops:
  24.9 1.2 %collective-permute-start = (f32[64,128]{1,0:T(8,128)S(1)}, f32[64,128]{1,0:T(8,128)S(1)}, u32[]{:S(2)}, u32[]{:S(2)}) collective-permute-start(f32[64,128]{1,0:T(8,128)S(1)} %get-tuple-element.49.near_ref), channel_id=1, source_target_pairs={{0,1},{1,0},{2,3},{3,2},{4,5},{5,4},{6,7},{7,6},{8,9},{9,8},{10,11... | collective-permute-start | bytes 98312 | tf_op jit(solution)/shard_map/ppermute | solution.py:305

commit v8 on v7

--- a/solution.py
+++ b/solution.py
@@ -122,9 +122,10 @@
     route_ref[...] = route(owners[...] == feat_index, holders, earlier, plan.home_slots, route_ref.shape)
     for flat, tall in ((grad, grad_tall), (hess, hess_tall)):
         values = flat[...].astype(jnp.float32)
-        for tile in range(row_count // LANES):
-            square = jnp.broadcast_to(values[tile : tile + 1], (LANES, LANES)).astype(jnp.bfloat16)
-            tall[tile * LANES : (tile + 1) * LANES, :] = square.T
+        for begin in range(0, row_count // LANES, 4):
+            tiles = [jnp.broadcast_to(values[at : at + 1], (LANES, LANES)) for at in range(begin, begin + 4)]
+            wide = jnp.concatenate(tiles, axis=1).astype(jnp.bfloat16)
+            tall[begin * LANES : (begin + 4) * LANES, :] = wide.T
     zero = jnp.zeros((HALF, CHUNK), jnp.bfloat16)
     one = jnp.ones((HALF, CHUNK), jnp.bfloat16)
 

time: 27.2 us -> 27.2 us (level)
  no operation moved by 1% of the time
where the time goes in v8:
time: 27.2 us; the launch traced here: 26.9 us
  blocking collectives  20.6 us (76%)
  Pallas kernels  4.43 us (16%)
  waiting for transfers between devices  0.97 us (4%)
  between operations  0.64 us (2%)
    all_to_all x1, blocking collectives, core_part(): lax.all_to_all(partial, 'row', split_axis=0, concat_axis=0, tiled=True, a...  11.3 us
    all_to_all x1, blocking collectives, core_part(): lax.all_to_all(outgoing, ('row', 'feat'), split_axis=0, concat_axis=0, ti...  9.29 us
    pallas_call x1, Pallas kernels, cut_sums(): pl.pallas_call(functools.partial(cut_sums_kernel, plan, start, count, per...  3.39 us
    ppermute x1, waiting for transfers between devices, shards(): far = lax.ppermute(near, 'feat', swap)  0.97 us
    pallas_call x1, Pallas kernels, shards(): pl.pallas_call(table_kernel, out_shape=(jax.ShapeDtypeStruct((plan.home_s...  0.77 us
  transfers between devices with their start and end apart: 1, of which 1 were waited for; matrix products, arithmetic and copies ran while one was open for 0% of the time, Pallas kernels for 0%

profile of v8, /device:TPU:0, one launch (start us, length us, event | category | flops | bytes accessed | tf_op | source)
XLA Modules:
  0.0 26.9 jit_solution(6165417396440341725)
XLA Ops:
  0.6 24.3 %conditional.1 = (f32[40,128]{1,0:T(8,128)S(1)}, f32[64,128]{1,0:T(8,128)S(1)}) conditional(s32[]{:T(128)} %convert_element_type.3, (s32[64,2]{0,1:T(2,128)}, bf16[8192]{0:T(1024)(128)(2,1)}, bf16[8192]{0:T(1024)(128)(2,1)}, s32[64]{0:T(128)}, s32[256,8192]{1,0:T(8,128)}) %tuple.21, (s32[64,2]{0,1:T(2,128)}, bf16[8192]{0:T(1024)(128)(2,1)}, ...), branch_computations={%region_0.1_spmd, %region_1.2_spmd} | conditional | bytes 458768 | solution.py:304
  0.7 3.4 %branch_1_fun.2 = (f32[8,16,128]{2,1,0:T(8,128)S(1)}, f32[40,128]{1,0:T(8,128)S(1)}) custom-call(s32[2,64]{1,0:T(2,128)} %bitcast.18, s32[256,8192]{1,0:T(8,128)} %get-tuple-element.31.codes_hbm, bf16[64,128]{1,0:T(8,128)(2,1)} %bitcast.14, bf16[64,128]{1,0:T(8,128)(2,1)} %bitcast.16, s32[1,64]{1,0:T(1,128)} %bitcast.20), custom_call_target="tpu_custom_call" | custom-call | tf_op jit(solution)/shard_map/cond/branch_1_fun/pallas_call | solution.py:180
  4.1 11.3 %all_to_all.18.parts_ref = f32[8,16,128]{2,1,0:T(8,128)S(1)} all-to-all(f32[8,16,128]{2,1,0:T(8,128)S(1)} %get-tuple-element.36), channel_id=1, replica_groups={{20,4,0,8,12,28,16,24},{21,5,1,9,13,29,17,25},{22,6,2,10,14,30,18,26},{..., dimensions={0} | all-to-all | bytes 131072 | tf_op jit(solution)/shard_map/cond/branch_1_fun/all_to_all | solution.py:283
  15.3 0.3 %branch_1_fun.3 = f32[16,4,128]{2,1,0:T(4,128)S(1)} custom-call(f32[8,16,128]{2,1,0:T(8,128)S(1)} %all_to_all.18.parts_ref), custom_call_target="tpu_custom_call" | custom-call | tf_op jit(solution)/shard_map/cond/branch_1_fun/pallas_call | solution.py:286
  15.6 9.3 %all_to_all.19 = f32[16,4,128]{2,1,0:T(4,128)S(1)} all-to-all(f32[16,4,128]{2,1,0:T(4,128)S(1)} %branch_1_fun.3), channel_id=1, replica_groups={{22,20,24,10,18,0,12,6,30,16,2,28,14,4,26,8},{23,21,25,11,19,1,13,7,31,..., dimensions={0} | all-to-all | bytes 65536 | tf_op jit(solution)/shard_map/cond/branch_1_fun/all_to_all | solution.py:294
  24.9 0.2 collective-permute-start
  25.2 1.0 %collective-permute-done.far_ref = f32[64,128]{1,0:T(8,128)S(1)} collective-permute-done((f32[64,128]{1,0:T(8,128)S(1)}, f32[64,128]{1,0:T(8,128)S(1)}, u32[]{:S(2)}, u32[]{:S(2)}) %collective-permute-start) | collective-permute-done | bytes 32800 | tf_op jit(solution)/shard_map/ppermute | solution.py:306
  26.1 0.8 %shard_map.68 = (f32[32,128]{1,0:T(8,128)}, f32[1,64]{1,0:T(1,128)}) custom-call(f32[40,128]{1,0:T(8,128)S(1)} %get-tuple-element.47.route_ref, f32[64,128]{1,0:T(8,128)S(1)} %get-tuple-element.49.near_ref, f32[64,128]{1,0:T(8,128)S(1)} %collective-permute-done.far_ref), custom_call_target="tpu_custom_call" | custom-call | tf_op jit(solution)/shard_map/pallas_call | solution.py:308
Async XLA Ops:
  24.9 1.2 %collective-permute-start = (f32[64,128]{1,0:T(8,128)S(1)}, f32[64,128]{1,0:T(8,128)S(1)}, u32[]{:S(2)}, u32[]{:S(2)}) collective-permute-start(f32[64,128]{1,0:T(8,128)S(1)} %get-tuple-element.49.near_ref), channel_id=1, source_target_pairs={{0,1},{1,0},{2,3},{3,2},{4,5},{5,4},{6,7},{7,6},{8,9},{9,8},{10,11... | collective-permute-start | bytes 98312 | tf_op jit(solution)/shard_map/ppermute | solution.py:306

commit v9 on v7

--- a/solution.py
+++ b/solution.py
@@ -17,7 +17,7 @@
 CHUNK = 2048
 HEAD = 5
 LATE_HEAD = 5
-ROW_ORDERS = {8: [5, 1, 0, 2, 3, 7, 4, 6]}
+ROW_ORDERS = {8: [5, 7, 0, 4, 3, 6, 1, 2]}
 MEMBER_ORDERS = {16: [11, 10, 12, 5, 9, 0, 6, 3, 15, 8, 1, 14, 7, 2, 13, 4]}
 SUMS_VMEM = 48 * 2**20
 SMALL_VMEM = 4 * 2**20

time: 27.2 us -> 27.4 us (level)
  no operation moved by 1% of the time
where the time goes in v9:
time: 27.4 us; the launch traced here: 27.1 us
  blocking collectives  20.7 us (76%)
  Pallas kernels  4.43 us (16%)
  waiting for transfers between devices  0.86 us (3%)
  between operations  0.64 us (2%)
  starting transfers between devices  0.4 us (1%)
    all_to_all x1, blocking collectives, core_part(): lax.all_to_all(partial, 'row', split_axis=0, concat_axis=0, tiled=True, a...  11.4 us
    all_to_all x1, blocking collectives, core_part(): lax.all_to_all(outgoing, ('row', 'feat'), split_axis=0, concat_axis=0, ti...  9.38 us
    pallas_call x1, Pallas kernels, cut_sums(): pl.pallas_call(functools.partial(cut_sums_kernel, plan, start, count, per...  3.39 us
    ppermute x1, waiting for transfers between devices, shards(): far = lax.ppermute(near, 'feat', swap)  0.86 us
    pallas_call x1, Pallas kernels, shards(): pl.pallas_call(table_kernel, out_shape=(jax.ShapeDtypeStruct((plan.home_s...  0.77 us
  transfers between devices with their start and end apart: 1, of which 1 were waited for; matrix products, arithmetic and copies ran while one was open for 0% of the time, Pallas kernels for 0%

profile of v9, /device:TPU:0, one launch (start us, length us, event | category | flops | bytes accessed | tf_op | source)
XLA Modules:
  0.0 27.1 jit_solution(18042176822202268784)
XLA Ops:
  0.6 24.4 %conditional.1 = (f32[40,128]{1,0:T(8,128)S(1)}, f32[64,128]{1,0:T(8,128)S(1)}) conditional(s32[]{:T(128)} %convert_element_type.3, (s32[64,2]{0,1:T(2,128)}, bf16[8192]{0:T(1024)(128)(2,1)}, bf16[8192]{0:T(1024)(128)(2,1)}, s32[64]{0:T(128)}, s32[256,8192]{1,0:T(8,128)}) %tuple.21, (s32[64,2]{0,1:T(2,128)}, bf16[8192]{0:T(1024)(128)(2,1)}, ...), branch_computations={%region_0.1_spmd, %region_1.2_spmd} | conditional | bytes 458768 | solution.py:303
  0.7 3.4 %branch_1_fun.2 = (f32[8,16,128]{2,1,0:T(8,128)S(1)}, f32[40,128]{1,0:T(8,128)S(1)}) custom-call(s32[2,64]{1,0:T(2,128)} %bitcast.18, s32[256,8192]{1,0:T(8,128)} %get-tuple-element.31.codes_hbm, bf16[64,128]{1,0:T(8,128)(2,1)} %bitcast.14, bf16[64,128]{1,0:T(8,128)(2,1)} %bitcast.16, s32[1,64]{1,0:T(1,128)} %bitcast.20), custom_call_target="tpu_custom_call" | custom-call | tf_op jit(solution)/shard_map/cond/branch_1_fun/pallas_call | solution.py:179
  4.1 11.4 %all_to_all.18.parts_ref = f32[8,16,128]{2,1,0:T(8,128)S(1)} all-to-all(f32[8,16,128]{2,1,0:T(8,128)S(1)} %get-tuple-element.36), channel_id=1, replica_groups={{20,28,0,16,12,24,4,8},{21,29,1,17,13,25,5,9},{22,30,2,18,14,26,6,10},{..., dimensions={0} | all-to-all | bytes 131072 | tf_op jit(solution)/shard_map/cond/branch_1_fun/all_to_all | solution.py:282
  15.4 0.3 %branch_1_fun.3 = f32[16,4,128]{2,1,0:T(4,128)S(1)} custom-call(f32[8,16,128]{2,1,0:T(8,128)S(1)} %all_to_all.18.parts_ref), custom_call_target="tpu_custom_call" | custom-call | tf_op jit(solution)/shard_map/cond/branch_1_fun/pallas_call | solution.py:285
  15.7 9.4 %all_to_all.19 = f32[16,4,128]{2,1,0:T(4,128)S(1)} all-to-all(f32[16,4,128]{2,1,0:T(4,128)S(1)} %branch_1_fun.3), channel_id=1, replica_groups={{22,20,24,10,18,0,12,6,30,16,2,28,14,4,26,8},{23,21,25,11,19,1,13,7,31,..., dimensions={0} | all-to-all | bytes 65536 | tf_op jit(solution)/shard_map/cond/branch_1_fun/all_to_all | solution.py:293
  25.1 0.4 %collective-permute-start = (f32[64,128]{1,0:T(8,128)S(1)}, f32[64,128]{1,0:T(8,128)S(1)}, u32[]{:S(2)}, u32[]{:S(2)}) collective-permute-start(f32[64,128]{1,0:T(8,128)S(1)} %get-tuple-element.49.near_ref), channel_id=1, source_target_pairs={{0,1},{1,0},{2,3},{3,2},{4,5},{5,4},{6,7},{7,6},{8,9},{9,8},{10,11... | collective-permute-start | bytes 98312 | tf_op jit(solution)/shard_map/ppermute | solution.py:305
  25.5 0.9 %collective-permute-done.far_ref = f32[64,128]{1,0:T(8,128)S(1)} collective-permute-done((f32[64,128]{1,0:T(8,128)S(1)}, f32[64,128]{1,0:T(8,128)S(1)}, u32[]{:S(2)}, u32[]{:S(2)}) %collective-permute-start) | collective-permute-done | bytes 32800 | tf_op jit(solution)/shard_map/ppermute | solution.py:305
  26.3 0.8 %shard_map.68 = (f32[32,128]{1,0:T(8,128)}, f32[1,64]{1,0:T(1,128)}) custom-call(f32[40,128]{1,0:T(8,128)S(1)} %get-tuple-element.47.route_ref, f32[64,128]{1,0:T(8,128)S(1)} %get-tuple-element.49.near_ref, f32[64,128]{1,0:T(8,128)S(1)} %collective-permute-done.far_ref), custom_call_target="tpu_custom_call" | custom-call | tf_op jit(solution)/shard_map/pallas_call | solution.py:307
Async XLA Ops:
  25.1 1.3 %collective-permute-start = (f32[64,128]{1,0:T(8,128)S(1)}, f32[64,128]{1,0:T(8,128)S(1)}, u32[]{:S(2)}, u32[]{:S(2)}) collective-permute-start(f32[64,128]{1,0:T(8,128)S(1)} %get-tuple-element.49.near_ref), channel_id=1, source_target_pairs={{0,1},{1,0},{2,3},{3,2},{4,5},{5,4},{6,7},{7,6},{8,9},{9,8},{10,11... | collective-permute-start | bytes 98312 | tf_op jit(solution)/shard_map/ppermute | solution.py:305
